TPU v7x, 512 devices: a whole 4x8x8 slice. The times are simulated.
512 devices in a mesh: seq: 64 (over z, y), head: 8 (over x, core).
Axes of the slice: x: 4, y: 8, z: 8, core: 2. Of those that a mesh axis runs over, the one named last changes fastest.
Arguments:
- query_rows: bfloat16 [16, 16384, 128], P('head', 'seq'), may hold values from -6 to 6
- key_rows: bfloat16 [16, 16384, 128], P('head', 'seq'), may hold values from -6 to 6
- value_rows: bfloat16 [16, 16384, 128], P('head', 'seq'), may hold values from -6 to 6
- norm_gain: float32 [16, 128], P('head'), may hold values from 0.25 to 1.75
- level_table: float32 [16, 16, 6], P(None, 'head'), may hold values from 0.3 to 4.5
- level_index: int32 [16384, 6], P('seq'), may hold values from 0 to 15
- window_length: int32 [16], P('head'), may hold values from 512 to 1024, as said below
- out_grad: bfloat16 [16, 16384, 128], P('head', 'seq'), may hold values from -18 to 18
Outputs:
- layer_out: bfloat16 [16, 16384, 128], P('head', 'seq')
- query_grad: bfloat16 [16, 16384, 128], P('head', 'seq')
- key_grad: bfloat16 [16, 16384, 128], P('head', 'seq')
- value_grad: bfloat16 [16, 16384, 128], P('head', 'seq')
- table_grad: float32 [16, 16, 6], P(None, 'head')
- gain_grad: float32 [16, 128], P('head')
Inputs may be any that keep to these rules, and one draw needn't show every extreme that they name: `window_length`: every head's window holds at least half of 1024 tokens and at most 1024; some head's window is exactly 1024.
All inputs are finite; a program needn't handle non-finite values.
Results may differ from a plain program's by a relative error of at most 0.0078.
Values may be sent and summed in bfloat16 or wider, within the bound.
A program may use at most 64 MiB of HBM per device.

v0:
```python
import functools
import math

import jax
import jax.numpy as jnp
from jax import lax
from jax.sharding import Mesh
from jax.sharding import PartitionSpec as P

H = 16
BLOCK = 64
WINDOW = 1024
LEVELS = 6
TABLE_ROWS = 16
SEQ = ("seq_0", "seq_1")


epsilon = 1e-06
block_cap = 512


def shifted(block, axis, distance):
    devices = range(lax.axis_size(axis))
    route = [(i - distance, i) for i in devices if i - distance in devices]
    return lax.ppermute(block, axis, route)


def from_partner(shard, axis, bit):
    return lax.ppermute(shard, axis, [(i, i ^ 1 << bit) for i in range(lax.axis_size(axis))])


def copy_for_each(shard, axis):
    copies = jnp.broadcast_to(shard, (lax.axis_size(axis), *shard.shape))
    return lax.all_to_all(copies, axis, split_axis=0, concat_axis=0, tiled=True)


def over_copies(shard, axis):
    everything = copy_for_each(shard, axis)
    return jnp.sum(everything, axis=0)


def as_sent(shard):

    def short(part):
        return part.astype(jnp.bfloat16) if part.dtype == jnp.float32 else part

    return jax.tree.map(short, shard)


def over_axes(shard, axes):
    return functools.reduce(lax.psum, axes, shard)


def contract(pattern, left_side, right_side):
    return jnp.einsum(pattern, left_side, right_side, preferred_element_type=jnp.float32)


def causal_mask():
    row_pos = lax.broadcasted_iota(jnp.int32, (BLOCK, BLOCK), 0)
    col_pos = lax.broadcasted_iota(jnp.int32, (BLOCK, BLOCK), 1)
    return row_pos >= col_pos


def window_mask(block_rows, shift_rows, key_count, span_len):
    query_pos = lax.broadcasted_iota(jnp.int32, (block_rows, key_count), 0)
    key_pos = lax.broadcasted_iota(jnp.int32, (block_rows, key_count), 1)
    offset = query_pos + shift_rows - key_pos
    return (offset >= 0) & (offset < span_len)


def leaf_view(tensor):
    head_count, token_count, head_dim = tensor.shape
    return tensor.reshape(head_count, token_count // BLOCK, BLOCK, head_dim)


def split_level(tensor, group_len):
    head_count, token_count, head_dim = tensor.shape
    return tensor.reshape(head_count, token_count // (2 * group_len), 2, group_len, head_dim)


def level_summary(key_rows, value_rows, group_len):
    lower_sum = contract(
        "hpse,hpsf->hpef",
        split_level(key_rows, group_len)[:, :, 0],
        split_level(value_rows, group_len)[:, :, 0],
    )
    return (lower_sum * (1.0 / math.sqrt(group_len * key_rows.shape[-1]))).astype(jnp.bfloat16)


def level_area(query_rows, summary, group_len):
    upper_half = contract("hpse,hpef->hpsf", split_level(query_rows, group_len)[:, :, 1], summary)
    return jnp.stack([jnp.zeros_like(upper_half), upper_half], axis=2).reshape(query_rows.shape)


def level_grads(query_rows, key_rows, value_rows, summary, upstream, group_len):
    upstream_up = split_level(upstream, group_len)[:, :, 1]
    query_up = contract("hpsf,hpef->hpse", upstream_up, summary)
    summary_grad = contract(
        "hpse,hpsf->hpef", split_level(query_rows, group_len)[:, :, 1], upstream_up
    )
    low_grad = (summary_grad * (1.0 / math.sqrt(group_len * query_rows.shape[-1]))).astype(
        jnp.bfloat16
    )
    key_low = contract("hpsf,hpef->hpse", split_level(value_rows, group_len)[:, :, 0], low_grad)
    value_low = contract("hpse,hpef->hpsf", split_level(key_rows, group_len)[:, :, 0], low_grad)
    blank = jnp.zeros_like(query_up)
    full_shape = query_rows.shape
    return (
        jnp.stack([blank, query_up], axis=2).reshape(full_shape),
        jnp.stack([key_low, blank], axis=2).reshape(full_shape),
        jnp.stack([value_low, blank], axis=2).reshape(full_shape),
    )


def window_head(query_head, key_head, value_head, span_len):
    token_count, head_dim = query_head.shape
    block_rows = min(block_cap, token_count)
    score_scale = lax.rsqrt((head_dim * span_len).astype(jnp.float32))
    inside = window_mask(block_rows, WINDOW, WINDOW + block_rows, span_len)
    scores = contract("qe,ke->qk", query_head, key_head) * score_scale
    prob_low = jnp.where(inside, scores, 0.0).astype(jnp.bfloat16)
    outputs = [contract("qk,ke->qe", prob_low, value_head)]
    return jnp.concatenate(outputs, axis=0)


def window_back_head(query_head, key_head, value_head, grad_head, span_len, keep_from):
    token_count, head_dim = query_head.shape
    block_rows = min(block_cap, token_count)
    score_scale = lax.rsqrt((head_dim * span_len).astype(jnp.float32))
    inside = window_mask(block_rows, WINDOW, WINDOW + block_rows, span_len)
    key_grad = jnp.zeros((WINDOW + token_count - keep_from, head_dim), jnp.float32)
    value_grad = jnp.zeros((WINDOW + token_count - keep_from, head_dim), jnp.float32)
    grad_part = grad_head[0:block_rows]
    scores = contract("qe,ke->qk", query_head, key_head) * score_scale
    prob_low = jnp.where(inside, scores, 0.0).astype(jnp.bfloat16)
    prob_grad = contract("qe,ke->qk", grad_part, value_head)
    score_grad = jnp.where(inside, prob_grad * score_scale, 0.0).astype(jnp.bfloat16)
    query_grad = [contract("qk,ke->qe", score_grad, key_head)]
    skip_cols = max(keep_from, 0)
    target = skip_cols - keep_from
    length_now = WINDOW + block_rows - skip_cols
    key_grad = key_grad.at[target : target + length_now].add(
        contract("qk,qe->ke", score_grad[:, skip_cols:], query_head)
    )
    value_grad = value_grad.at[target : target + length_now].add(
        contract("qk,qe->ke", prob_low, grad_part)
    )
    return (jnp.concatenate(query_grad, axis=0), key_grad, value_grad)


def shards(
    query_rows, key_rows, value_rows, norm_gain, level_table, level_index, window_length, out_grad
):
    heads_here, tok_here, head_dim = query_rows.shape
    seq_index = lax.axis_index(SEQ)
    seq_levels = lax.axis_size(SEQ).bit_length() - 1
    local_levels = (tok_here // BLOCK).bit_length() - 1
    reach_count = WINDOW // tok_here
    onehot = (
        level_index[:, :, None] == lax.broadcasted_iota(jnp.int32, (1, 1, TABLE_ROWS), 2)
    ).astype(jnp.float32)
    weights = jnp.einsum("tjk,khj->htj", onehot, level_table, precision=lax.Precision.HIGHEST)

    def weight_of(level_no):
        return weights[:, :, min(level_no, LEVELS - 1)][:, :, None]

    own_pair = jnp.stack([key_rows, value_rows])
    pieces = []
    for step_no in range(reach_count, 0, -1):
        pieces.append(shifted(own_pair, SEQ, step_no))
    pieces.append(own_pair)
    wide_pair = jnp.concatenate(pieces, axis=2)
    device_summary = contract("hte,htf->hef", key_rows, value_rows)
    sibling = []
    running = device_summary
    for bit_no in range(seq_levels):
        partner = from_partner(running, SEQ, bit_no)
        upper_half = seq_index >> bit_no & 1 == 1
        sibling.append(jnp.where(upper_half, partner, 0.0))
        running = running + partner
    query_leaf = leaf_view(query_rows)
    key_leaf = leaf_view(key_rows)
    value_leaf = leaf_view(value_rows)
    leaf_scale = 1.0 / math.sqrt(BLOCK * head_dim)
    causal = causal_mask()
    leaf_prob = jnp.where(
        causal, contract("hcte,hcse->hcts", query_leaf, key_leaf) * leaf_scale, 0.0
    ).astype(jnp.bfloat16)
    area_list = [contract("hcts,hcse->hcte", leaf_prob, value_leaf).reshape(query_rows.shape)]
    summaries = []
    for level_no in range(1, local_levels + 1):
        group_len = BLOCK * 2 ** (level_no - 1)
        summary = level_summary(key_rows, value_rows, group_len)
        summaries.append(summary)
        area_list.append(level_area(query_rows, summary, group_len))
    for bit_no in range(seq_levels):
        group_len = tok_here * 2**bit_no
        summary = (sibling[bit_no] * (1.0 / math.sqrt(group_len * head_dim))).astype(jnp.bfloat16)
        summaries.append(summary)
        area_list.append(contract("hte,hef->htf", query_rows, summary))
    mixed = lax.map(
        lambda head_items: window_head(head_items[0], head_items[1], head_items[2], head_items[3]),
        (query_rows, wide_pair[0], wide_pair[1], window_length),
    )
    for level_no in range(len(area_list)):
        mixed = mixed + weight_of(level_no) * area_list[level_no]
    grad_full = out_grad.astype(jnp.float32)
    scaled = grad_full * norm_gain[:, None, :]
    square_sum, cross_sum = (
        over_copies(jnp.sum(mixed * mixed, axis=(0, 2)), "head"),
        over_copies(jnp.sum(scaled * mixed, axis=(0, 2)), "head"),
    )
    inv_rms = lax.rsqrt(square_sum / (H * head_dim) + epsilon)
    layer_out = (mixed * inv_rms[None, :, None] * norm_gain[:, None, :]).astype(jnp.bfloat16)
    mixed_grad = (
        scaled * inv_rms[None, :, None]
        - mixed * (inv_rms**3 * cross_sum / (H * head_dim))[None, :, None]
    )
    gain_part = jnp.sum(grad_full * mixed * inv_rms[None, :, None], axis=1)
    grad_low = mixed_grad.astype(jnp.bfloat16)
    columns = [jnp.zeros((heads_here, tok_here), jnp.float32) for column_no in range(LEVELS)]
    for level_no in range(len(area_list)):
        column_no = min(level_no, LEVELS - 1)
        columns[column_no] = columns[column_no] + jnp.sum(mixed_grad * area_list[level_no], axis=2)
    upstream_leaf = leaf_view((weight_of(0) * mixed_grad).astype(jnp.bfloat16))
    prob_grad = contract("hcte,hcse->hcts", upstream_leaf, value_leaf)
    score_grad = jnp.where(causal, prob_grad * leaf_scale, 0.0).astype(jnp.bfloat16)
    query_grad = contract("hcts,hcse->hcte", score_grad, key_leaf).reshape(query_rows.shape)
    key_grad = contract("hcts,hcte->hcse", score_grad, query_leaf).reshape(query_rows.shape)
    value_grad = contract("hcts,hcte->hcse", leaf_prob, upstream_leaf).reshape(query_rows.shape)
    for level_no in range(1, local_levels + 1):
        group_len = BLOCK * 2 ** (level_no - 1)
        upstream = (weight_of(level_no) * mixed_grad).astype(jnp.bfloat16)
        query_part, key_part, value_part = level_grads(
            query_rows, key_rows, value_rows, summaries[level_no - 1], upstream, group_len
        )
        query_grad = query_grad + query_part
        key_grad = key_grad + key_part
        value_grad = value_grad + value_part
    summary_grads = []
    for bit_no in range(seq_levels):
        level_no = local_levels + 1 + bit_no
        upstream = (weight_of(level_no) * mixed_grad).astype(jnp.bfloat16)
        query_grad = query_grad + contract("htf,hef->hte", upstream, summaries[level_no - 1])
        group_len = tok_here * 2**bit_no
        partial_value = contract("hte,htf->hef", query_rows, upstream) * (
            1.0 / math.sqrt(group_len * head_dim)
        )
        upper_half = seq_index >> bit_no & 1 == 1
        summary_grads.append(jnp.where(upper_half, partial_value, 0.0))
    pending = jnp.stack(summary_grads)
    for bit_no in range(seq_levels):
        partner = from_partner(as_sent(pending[bit_no:]), SEQ, bit_no)
        lower_half = seq_index >> bit_no & 1 == 0
        received = jnp.where(lower_half, partner[0], 0.0).astype(jnp.bfloat16)
        key_grad = key_grad + contract("htf,hef->hte", value_rows, received)
        value_grad = value_grad + contract("hte,hef->htf", key_rows, received)
        pending = jnp.concatenate(
            [pending[: bit_no + 1], pending[bit_no + 1 :] + partner[1:]], axis=0
        )
    keep_from = 0
    window_query, window_key, window_value = lax.map(
        lambda head_items: window_back_head(
            head_items[0], head_items[1], head_items[2], head_items[3], head_items[4], keep_from
        ),
        (query_rows, wide_pair[0], wide_pair[1], grad_low, window_length),
    )
    query_grad = query_grad + window_query
    key_grad = key_grad + window_key[:, WINDOW:]
    value_grad = value_grad + window_value[:, WINDOW:]
    for step_no in range(1, reach_count + 1):
        first_row = (reach_count - step_no) * tok_here
        piece = jnp.stack(
            [
                window_key[:, first_row : first_row + tok_here],
                window_value[:, first_row : first_row + tok_here],
            ]
        )
        arrived = shifted(piece.astype(jnp.bfloat16), SEQ, -step_no).astype(piece.dtype)
        key_grad = key_grad + arrived[0]
        value_grad = value_grad + arrived[1]
    weight_grad = jnp.stack(columns, axis=-1)
    table_part = jnp.einsum("tjk,htj->khj", onehot, weight_grad, precision=lax.Precision.HIGHEST)
    table_grad, gain_grad = (over_axes(table_part, SEQ), over_axes(gain_part, SEQ))
    return (
        layer_out,
        query_grad.astype(jnp.bfloat16),
        key_grad.astype(jnp.bfloat16),
        value_grad.astype(jnp.bfloat16),
        table_grad,
        gain_grad,
    )


def solution(mesh):
    torus = Mesh(mesh.devices.reshape(8, 8, mesh.shape["head"]), ("seq_0", "seq_1", "head"))
    placed = (
        P("head", SEQ, None),
        P("head", SEQ, None),
        P("head", SEQ, None),
        P("head", None),
        P(None, "head", None),
        P(SEQ, None),
        P("head"),
        P("head", SEQ, None),
    )
    return jax.shard_map(
        shards,
        mesh=torus,
        in_specs=placed,
        out_specs=(
            P("head", SEQ, None),
            P("head", SEQ, None),
            P("head", SEQ, None),
            P("head", SEQ, None),
            P(None, "head", None),
            P("head", None),
        ),
        check_vma=False,
    )
```

profile of v0, /device:TPU:56, one launch (start us, length us, event | category | flops | bytes accessed | tf_op | source)
XLA Modules:
  0.0 325.4 jit_solution(17275085124501058905)
XLA Ops:
  1.7 6.5 %collective-permute-start = (bf16[2,2,256,128]{3,2,1,0:T(8,128)(2,1)S(1)}, bf16[2,2,256,128]{3,2,1,0:T(8,128)(2,1)}, u32[]{:S(2)}, u32[]{:S(2)}) collective-permute-start(bf16[2,2,256,128]{3,2,1,0:T(8,128)(2,1)S(1)} %pad_maximum_fusion), channel_id=1, source_target_pairs={{0,32},{8,40},{16,48},{24,56},{32,64},{40,72},{48,80},{56,88},{64,... | collective-permute-start | bytes 786440 | tf_op jit(solution)/shard_map/ppermute | solution.py:25
  8.3 4.9 %collective-permute-start.1 = (bf16[2,2,256,128]{3,2,1,0:T(8,128)(2,1)S(1)}, bf16[2,2,256,128]{3,2,1,0:T(8,128)(2,1)}, u32[]{:S(2)}, u32[]{:S(2)}) collective-permute-start(bf16[2,2,256,128]{3,2,1,0:T(8,128)(2,1)S(1)} %pad_maximum_fusion), channel_id=1, source_target_pairs={{0,24},{8,32},{16,40},{24,48},{32,56},{40,64},{48,72},{56,80},{64,... | collective-permute-start | bytes 786440 | tf_op jit(solution)/shard_map/ppermute | solution.py:25
  13.2 3.6 %collective-permute-start.2 = (bf16[2,2,256,128]{3,2,1,0:T(8,128)(2,1)S(1)}, bf16[2,2,256,128]{3,2,1,0:T(8,128)(2,1)S(1)}, u32[]{:S(2)}, u32[]{:S(2)}) collective-permute-start(bf16[2,2,256,128]{3,2,1,0:T(8,128)(2,1)S(1)} %pad_maximum_fusion), channel_id=1, source_target_pairs={{0,16},{8,24},{16,32},{24,40},{32,48},{40,56},{48,64},{56,72},{64,... | collective-permute-start | bytes 786440 | tf_op jit(solution)/shard_map/ppermute | solution.py:25
  16.8 3.5 %collective-permute-start.3 = (bf16[2,2,256,128]{3,2,1,0:T(8,128)(2,1)S(1)}, bf16[2,2,256,128]{3,2,1,0:T(8,128)(2,1)S(1)}, u32[]{:S(2)}, u32[]{:S(2)}) collective-permute-start(bf16[2,2,256,128]{3,2,1,0:T(8,128)(2,1)S(1)} %pad_maximum_fusion), channel_id=1, source_target_pairs={{0,8},{8,16},{16,24},{24,32},{32,40},{40,48},{48,56},{56,64},{64,7... | collective-permute-start | bytes 786440 | tf_op jit(solution)/shard_map/ppermute | solution.py:25
  20.3 1.2 fusion.202
  21.5 2.4 collective-permute-start.4
  25.4 1.1 fusion.104
  26.5 1.1 fusion.94
  29.1 27.5 %collective-permute-done.4 = f32[2,128,128]{2,1,0:T(8,128)S(1)} collective-permute-done((f32[2,128,128]{2,1,0:T(8,128)S(1)}, f32[2,128,128]{2,1,0:T(8,128)S(1)}, u32[]{:S(2)}, u32[]{:S(2)}) %collective-permute-start.4) | collective-permute-done | bytes 131104 | tf_op jit(solution)/shard_map/ppermute | solution.py:29
  56.6 2.5 collective-permute-start.5
  59.4 7.2 %collective-permute-done.5 = f32[2,128,128]{2,1,0:T(8,128)S(1)} collective-permute-done((f32[2,128,128]{2,1,0:T(8,128)S(1)}, f32[2,128,128]{2,1,0:T(8,128)S(1)}, u32[]{:S(2)}, u32[]{:S(2)}) %collective-permute-start.5) | collective-permute-done | bytes 131104 | tf_op jit(solution)/shard_map/ppermute | solution.py:29
  66.7 3.3 %collective-permute-start.6 = (f32[2,128,128]{2,1,0:T(8,128)S(1)}, f32[2,128,128]{2,1,0:T(8,128)S(1)}, u32[]{:S(2)}, u32[]{:S(2)}) collective-permute-start(f32[2,128,128]{2,1,0:T(8,128)S(1)} %add.288), channel_id=1, source_target_pairs={{0,32},{8,40},{16,48},{24,56},{32,0},{40,8},{48,16},{56,24},{64,96... | collective-permute-start | bytes 393224 | tf_op jit(solution)/shard_map/ppermute | solution.py:29
  73.1 8.5 %while.31 = (s32[]{:T(128)}, f32[2,256,128]{1,2,0:T(8,128)}, s32[2]{0:T(128)S(1)}, bf16[2,256,128]{2,1,0:T(8,128)(2,1)S(1)}, bf16[2,1280,128]{2,1,0:T(8,128)(2,1...) while((s32[]{:T(128)}, f32[2,256,128]{1,2,0:T(8,128)}, s32[2]{0:T(128)S(1)}, ...), condition=%wide.region_1.2_spmd, body=%wide.region_0.1_spmd.sunk | while | flops 170066176 | bytes 857221 | solution.py:201
  74.4 3.0 fusion.278
  78.6 3.0 fusion.278
  81.9 4.3 %collective-permute-start.7 = (f32[2,128,128]{2,1,0:T(8,128)S(1)}, f32[2,128,128]{2,1,0:T(8,128)S(1)}, u32[]{:S(2)}, u32[]{:S(2)}) collective-permute-start(f32[2,128,128]{2,1,0:T(8,128)S(1)} %add.290), channel_id=1, source_target_pairs={{0,64},{8,72},{16,80},{24,88},{32,96},{40,104},{48,112},{56,120},{... | collective-permute-start | bytes 393224 | tf_op jit(solution)/shard_map/ppermute | solution.py:29
  86.4 2.7 collective-permute-done.7
  89.1 6.1 %collective-permute-start.8 = (f32[2,128,128]{2,1,0:T(8,128)S(1)}, f32[2,128,128]{2,1,0:T(8,128)S(1)}, u32[]{:S(2)}, u32[]{:S(2)}) collective-permute-start(f32[2,128,128]{2,1,0:T(8,128)S(1)} %add.292), channel_id=1, source_target_pairs={{0,128},{8,136},{16,144},{24,152},{32,160},{40,168},{48,176},{56,1... | collective-permute-start | bytes 393224 | tf_op jit(solution)/shard_map/ppermute | solution.py:29
  95.5 4.6 %collective-permute-done.8 = f32[2,128,128]{2,1,0:T(8,128)S(1)} collective-permute-done((f32[2,128,128]{2,1,0:T(8,128)S(1)}, f32[2,128,128]{2,1,0:T(8,128)S(1)}, u32[]{:S(2)}, u32[]{:S(2)}) %collective-permute-start.8) | collective-permute-done | bytes 131104 | tf_op jit(solution)/shard_map/ppermute | solution.py:29
  100.2 9.5 %collective-permute-start.9 = (f32[2,128,128]{2,1,0:T(8,128)S(1)}, f32[2,128,128]{2,1,0:T(8,128)S(1)}, u32[]{:S(2)}, u32[]{:S(2)}) collective-permute-start(f32[2,128,128]{2,1,0:T(8,128)S(1)} %add.294), channel_id=1, source_target_pairs={{0,256},{8,264},{16,272},{24,280},{32,288},{40,296},{48,304},{56,3... | collective-permute-start | bytes 393224 | tf_op jit(solution)/shard_map/ppermute | solution.py:29
  109.9 4.1 %collective-permute-done.9 = f32[2,128,128]{2,1,0:T(8,128)S(1)} collective-permute-done((f32[2,128,128]{2,1,0:T(8,128)S(1)}, f32[2,128,128]{2,1,0:T(8,128)S(1)}, u32[]{:S(2)}, u32[]{:S(2)}) %collective-permute-start.9) | collective-permute-done | bytes 131104 | tf_op jit(solution)/shard_map/ppermute | solution.py:29
  114.0 1.9 multiply_reduce_fusion.9
  116.6 4.3 %all-to-all-start = ((f32[8,1,256]{2,1,0:T(1,128)}), f32[8,1,256]{2,1,0:T(1,128)}, u32[]{:S(2)}, u32[]{:S(2)}) async-start(f32[8,1,256]{2,1,0:T(1,128)} %broadcast_in_dim.80), calls=%async_computation | async-start | bytes 16384 | tf_op jit(solution)/shard_map/all_to_all | solution.py:34
  120.9 1.7 copy.201
  122.6 3.8 %all-to-all-done = f32[8,1,256]{2,1,0:T(1,128)} async-done(((f32[8,1,256]{2,1,0:T(1,128)}), f32[8,1,256]{2,1,0:T(1,128)}, u32[]{:S(2)}, u32[]{:S(2)}) %all-to-all-start) | async-done | bytes 8224 | tf_op jit(solution)/shard_map/all_to_all | solution.py:34
  126.3 1.3 reduce_sum.127
  128.9 1.7 fusion.113
  131.1 3.9 %all-to-all-start.1 = ((f32[8,1,256]{2,1,0:T(1,128)}), f32[8,1,256]{2,1,0:T(1,128)}, u32[]{:S(2)}, u32[]{:S(2)}) async-start(f32[8,1,256]{2,1,0:T(1,128)} %broadcast_in_dim.81), calls=%async_computation.1 | async-start | bytes 16384 | tf_op jit(solution)/shard_map/all_to_all | solution.py:34
  135.1 5.2 %all-to-all-done.1 = f32[8,1,256]{2,1,0:T(1,128)} async-done(((f32[8,1,256]{2,1,0:T(1,128)}), f32[8,1,256]{2,1,0:T(1,128)}, u32[]{:S(2)}, u32[]{:S(2)}) %all-to-all-start.1) | async-done | bytes 8224 | tf_op jit(solution)/shard_map/all_to_all | solution.py:34
  140.4 1.3 reduce_sum.129
  142.4 2.7 multiply_reduce_fusion.2
  149.6 1.7 convolution_bitcast_fusion.28
  151.3 1.1 fusion.96
  155.0 1.7 copy.242
  156.7 16.3 %while.32 = (s32[]{:T(128)}, f32[2,256,128]{2,1,0:T(8,128)}, f32[2,1280,128]{1,2,0:T(8,128)S(1)}, f32[2,1280,128]{1,2,0:T(8,128)}, s32[2]{0:T(128)}, /*index=5*/...) while((s32[]{:T(128)}, f32[2,256,128]{2,1,0:T(8,128)}, ...), condition=%wide.region_7.8_spmd, body=%wide.region_6.7_spmd.sunk | while | flops 424018176 | bytes 6764785 | solution.py:262
  156.7 1.2 dynamic_slice.117
  158.7 2.2 fusion.288
  161.9 2.9 fusion.291
  164.8 1.2 dynamic_slice.117
  166.8 2.2 fusion.288
  170.1 2.9 fusion.291
  173.0 1.8 stack.159.clone
  174.8 1.6 stack.157.clone
  182.9 1.9 collective-permute-start.10
  186.8 6.2 %collective-permute-start.19 = (bf16[2,2,256,128]{2,3,1,0:T(8,128)(2,1)}, bf16[2,2,256,128]{2,3,1,0:T(8,128)(2,1)}, u32[]{:S(2)}, u32[]{:S(2)}) collective-permute-start(bf16[2,2,256,128]{2,3,1,0:T(8,128)(2,1)} %pad_maximum_fusion.4), channel_id=1, source_target_pairs={{32,0},{40,8},{48,16},{56,24},{64,32},{72,40},{80,48},{88,56},{96,... | collective-permute-start | bytes 786440 | tf_op jit(solution)/shard_map/ppermute | solution.py:25
  193.6 3.0 collective-permute-start.18
  197.5 2.2 collective-permute-start.17
  200.4 2.5 collective-permute-start.16
  207.8 23.4 %all-reduce.9 = (f32[16,2,6]{0,1,2:T(2,128)S(1)}, f32[2,128]{1,0:T(2,128)S(1)}) all-reduce(f32[16,2,6]{0,1,2:T(2,128)S(1)} %convolution_bitcast_fusion.30, f32[2,128]{1,0:T(2,128)S(1)} %copy-done.60), channel_id=1, replica_groups=mesh['seq_0'=8,'seq_1'=8,'head'=8] {'seq_0'}, use_global_device_ids=true, to_apply=%region_17.18 | all-reduce | flops 448 | bytes 3584 | tf_op jit(solution)/shard_map/psum | solution.py:51
  231.3 20.3 %all-reduce.8 = (f32[16,2,6]{0,1,2:T(2,128)}, f32[2,128]{1,0:T(2,128)}) all-reduce(f32[16,2,6]{0,1,2:T(2,128)S(1)} %get-tuple-element.332, f32[2,128]{1,0:T(2,128)S(1)} %get-tuple-element.333), channel_id=1, replica_groups=mesh['seq_0'=8,'seq_1'=8,'head'=8] {'seq_1'}, use_global_device_ids=true, to_apply=%region_18.19 | all-reduce | flops 448 | bytes 3584 | tf_op jit(solution)/shard_map/psum | solution.py:51
  256.7 1.1 fusion.200
  257.8 4.6 %collective-permute-start.11 = (bf16[5,2,128,128]{2,3,1,0:T(8,128)(2,1)S(1)}, bf16[5,2,128,128]{2,3,1,0:T(8,128)(2,1)S(1)}, u32[]{:S(2)}, u32[]{:S(2)}) collective-permute-start(bf16[5,2,128,128]{2,3,1,0:T(8,128)(2,1)S(1)} %get-tuple-element.341), channel_id=1, source_target_pairs={{0,16},{8,24},{16,0},{24,8},{32,48},{40,56},{48,32},{56,40},{64,80... | collective-permute-start | bytes 983048 | tf_op jit(solution)/shard_map/ppermute | solution.py:29
  262.4 1.1 fusion.85
  264.6 9.0 %collective-permute-done.11 = bf16[5,2,128,128]{2,3,1,0:T(8,128)(2,1)S(1)} collective-permute-done((bf16[5,2,128,128]{2,3,1,0:T(8,128)(2,1)S(1)}, bf16[5,2,128,128]{2,3,1,0:T(8,128)(2,1)S(1)}, u32[]{:S(2)}, u32[]{:S(2)}) %collective-permute-start.11) | collective-permute-done | bytes 327712 | tf_op jit(solution)/shard_map/ppermute | solution.py:29
  273.7 5.0 %collective-permute-start.12 = (bf16[4,2,128,128]{2,3,1,0:T(8,128)(2,1)S(1)}, bf16[4,2,128,128]{2,3,1,0:T(8,128)(2,1)S(1)}, u32[]{:S(2)}, u32[]{:S(2)}) collective-permute-start(bf16[4,2,128,128]{2,3,1,0:T(8,128)(2,1)S(1)} %get-tuple-element.339), channel_id=1, source_target_pairs={{0,32},{8,40},{16,48},{24,56},{32,0},{40,8},{48,16},{56,24},{64,96... | collective-permute-start | bytes 786440 | tf_op jit(solution)/shard_map/ppermute | solution.py:29
  279.1 13.0 %collective-permute-done.12 = bf16[4,2,128,128]{2,3,1,0:T(8,128)(2,1)S(1)} collective-permute-done((bf16[4,2,128,128]{2,3,1,0:T(8,128)(2,1)S(1)}, bf16[4,2,128,128]{2,3,1,0:T(8,128)(2,1)S(1)}, u32[]{:S(2)}, u32[]{:S(2)}) %collective-permute-start.12) | collective-permute-done | bytes 262176 | tf_op jit(solution)/shard_map/ppermute | solution.py:29
  292.2 1.9 collective-permute-start.13
  294.6 6.3 %collective-permute-done.13 = bf16[3,2,128,128]{2,3,1,0:T(8,128)(2,1)S(1)} collective-permute-done((bf16[3,2,128,128]{2,3,1,0:T(8,128)(2,1)S(1)}, bf16[3,2,128,128]{2,3,1,0:T(8,128)(2,1)S(1)}, u32[]{:S(2)}, u32[]{:S(2)}) %collective-permute-start.13) | collective-permute-done | bytes 196640 | tf_op jit(solution)/shard_map/ppermute | solution.py:29
  301.0 2.0 collective-permute-start.14
  303.5 7.7 %collective-permute-done.14 = bf16[2,2,128,128]{2,3,1,0:T(8,128)(2,1)S(1)} collective-permute-done((bf16[2,2,128,128]{2,3,1,0:T(8,128)(2,1)S(1)}, bf16[2,2,128,128]{2,3,1,0:T(8,128)(2,1)S(1)}, u32[]{:S(2)}, u32[]{:S(2)}) %collective-permute-start.14) | collective-permute-done | bytes 131104 | tf_op jit(solution)/shard_map/ppermute | solution.py:29
  311.2 8.0 %collective-permute-start.15 = (bf16[1,2,128,128]{2,3,1,0:T(8,128)(2,1)S(1)}, bf16[1,2,128,128]{2,3,1,0:T(8,128)(2,1)S(1)}, u32[]{:S(2)}, u32[]{:S(2)}) collective-permute-start(bf16[1,2,128,128]{2,3,1,0:T(8,128)(2,1)S(1)} %fusion.115), channel_id=1, source_target_pairs={{0,256},{8,264},{16,272},{24,280},{32,288},{40,296},{48,304},{56,3... | collective-permute-start | bytes 196616 | tf_op jit(solution)/shard_map/ppermute | solution.py:29
  319.6 1.8 collective-permute-done.15
  321.4 1.2 fusion.99
  323.4 1.2 fusion.98
  (269 shorter events, 46.2 us)
Async XLA Ops:
  0.6 23.2 %copy-start = (f32[16,2,6]{0,1,2:T(2,128)S(1)}, f32[16,2,6]{0,1,2:T(2,128)}, u32[]{:S(2)}) copy-start(f32[16,2,6]{0,1,2:T(2,128)} %param.24) | copy-start | bytes 2308
  0.6 27.2 %copy-start.2 = (bf16[2,256,128]{2,1,0:T(8,128)(2,1)S(1)}, bf16[2,256,128]{2,1,0:T(8,128)(2,1)}, u32[]{:S(2)}) copy-start(bf16[2,256,128]{2,1,0:T(8,128)(2,1)} %param.22) | copy-start | bytes 393220
  0.7 27.0 %copy-start.3 = (bf16[2,256,128]{2,1,0:T(8,128)(2,1)S(1)}, bf16[2,256,128]{2,1,0:T(8,128)(2,1)}, u32[]{:S(2)}) copy-start(bf16[2,256,128]{2,1,0:T(8,128)(2,1)} %param.21) | copy-start | bytes 393220
  0.7 27.0 %copy-start.1 = (bf16[2,256,128]{2,1,0:T(8,128)(2,1)S(1)}, bf16[2,256,128]{2,1,0:T(8,128)(2,1)}, u32[]{:S(2)}) copy-start(bf16[2,256,128]{2,1,0:T(8,128)(2,1)} %param.20) | copy-start | bytes 393220
  1.7 68.3 %collective-permute-start = (bf16[2,2,256,128]{3,2,1,0:T(8,128)(2,1)S(1)}, bf16[2,2,256,128]{3,2,1,0:T(8,128)(2,1)}, u32[]{:S(2)}, u32[]{:S(2)}) collective-permute-start(bf16[2,2,256,128]{3,2,1,0:T(8,128)(2,1)S(1)} %pad_maximum_fusion), channel_id=1, source_target_pairs={{0,32},{8,40},{16,48},{24,56},{32,64},{40,72},{48,80},{56,88},{64,... | collective-permute-start | bytes 786440 | tf_op jit(solution)/shard_map/ppermute | solution.py:25
  8.3 62.7 %collective-permute-start.1 = (bf16[2,2,256,128]{3,2,1,0:T(8,128)(2,1)S(1)}, bf16[2,2,256,128]{3,2,1,0:T(8,128)(2,1)}, u32[]{:S(2)}, u32[]{:S(2)}) collective-permute-start(bf16[2,2,256,128]{3,2,1,0:T(8,128)(2,1)S(1)} %pad_maximum_fusion), channel_id=1, source_target_pairs={{0,24},{8,32},{16,40},{24,48},{32,56},{40,64},{48,72},{56,80},{64,... | collective-permute-start | bytes 786440 | tf_op jit(solution)/shard_map/ppermute | solution.py:25
  13.2 58.8 %collective-permute-start.2 = (bf16[2,2,256,128]{3,2,1,0:T(8,128)(2,1)S(1)}, bf16[2,2,256,128]{3,2,1,0:T(8,128)(2,1)S(1)}, u32[]{:S(2)}, u32[]{:S(2)}) collective-permute-start(bf16[2,2,256,128]{3,2,1,0:T(8,128)(2,1)S(1)} %pad_maximum_fusion), channel_id=1, source_target_pairs={{0,16},{8,24},{16,32},{24,40},{32,48},{40,56},{48,64},{56,72},{64,... | collective-permute-start | bytes 786440 | tf_op jit(solution)/shard_map/ppermute | solution.py:25
  16.8 55.2 %collective-permute-start.3 = (bf16[2,2,256,128]{3,2,1,0:T(8,128)(2,1)S(1)}, bf16[2,2,256,128]{3,2,1,0:T(8,128)(2,1)S(1)}, u32[]{:S(2)}, u32[]{:S(2)}) collective-permute-start(bf16[2,2,256,128]{3,2,1,0:T(8,128)(2,1)S(1)} %pad_maximum_fusion), channel_id=1, source_target_pairs={{0,8},{8,16},{16,24},{24,32},{32,40},{40,48},{48,56},{56,64},{64,7... | collective-permute-start | bytes 786440 | tf_op jit(solution)/shard_map/ppermute | solution.py:25
  21.5 35.1 %collective-permute-start.4 = (f32[2,128,128]{2,1,0:T(8,128)S(1)}, f32[2,128,128]{2,1,0:T(8,128)S(1)}, u32[]{:S(2)}, u32[]{:S(2)}) collective-permute-start(f32[2,128,128]{2,1,0:T(8,128)S(1)} %fusion.202), channel_id=1, source_target_pairs={{0,8},{8,0},{16,24},{24,16},{32,40},{40,32},{48,56},{56,48},{64,72... | collective-permute-start | bytes 393224 | tf_op jit(solution)/shard_map/ppermute | solution.py:29
  23.9 4.9 %copy-start.49 = (pred[64,64]{1,0:T(8,128)(4,1)}, pred[64,64]{1,0:T(8,128)(4,1)S(1)}, u32[]{:S(2)}) copy-start(pred[64,64]{1,0:T(8,128)(4,1)S(1)} %iota_compare_fusion.3) | copy-start | bytes 12292
  56.6 10.0 %collective-permute-start.5 = (f32[2,128,128]{2,1,0:T(8,128)S(1)}, f32[2,128,128]{2,1,0:T(8,128)S(1)}, u32[]{:S(2)}, u32[]{:S(2)}) collective-permute-start(f32[2,128,128]{2,1,0:T(8,128)S(1)} %add.286), channel_id=1, source_target_pairs={{0,16},{8,24},{16,0},{24,8},{32,48},{40,56},{48,32},{56,40},{64,80... | collective-permute-start | bytes 393224 | tf_op jit(solution)/shard_map/ppermute | solution.py:29
  66.6 15.0 %copy-start.14 = (f32[2,128,128]{2,1,0:T(8,128)}, f32[2,128,128]{2,1,0:T(8,128)S(1)}, u32[]{:S(2)}) copy-start(f32[2,128,128]{2,1,0:T(8,128)S(1)} %collective-permute-done.5) | copy-start | bytes 393220
  66.7 15.2 %collective-permute-start.6 = (f32[2,128,128]{2,1,0:T(8,128)S(1)}, f32[2,128,128]{2,1,0:T(8,128)S(1)}, u32[]{:S(2)}, u32[]{:S(2)}) collective-permute-start(f32[2,128,128]{2,1,0:T(8,128)S(1)} %add.288), channel_id=1, source_target_pairs={{0,32},{8,40},{16,48},{24,56},{32,0},{40,8},{48,16},{56,24},{64,96... | collective-permute-start | bytes 393224 | tf_op jit(solution)/shard_map/ppermute | solution.py:29
  81.8 32.2 %copy-start.40 = (f32[2,256]{1,0:T(2,128)S(1)}, f32[2,256]{1,0:T(2,128)}, u32[]{:S(2)}) copy-start(f32[2,256]{1,0:T(2,128)} %get-tuple-element.361) | copy-start | bytes 6148
  81.8 32.2 %copy-start.42 = (f32[2,256]{1,0:T(2,128)S(1)}, f32[2,256]{1,0:T(2,128)}, u32[]{:S(2)}) copy-start(f32[2,256]{1,0:T(2,128)} %get-tuple-element.362) | copy-start | bytes 6148
  81.8 32.2 %copy-start.44 = (f32[2,256]{1,0:T(2,128)S(1)}, f32[2,256]{1,0:T(2,128)}, u32[]{:S(2)}) copy-start(f32[2,256]{1,0:T(2,128)} %get-tuple-element.365) | copy-start | bytes 6148
  81.9 32.2 %copy-start.46 = (f32[2,256]{1,0:T(2,128)S(1)}, f32[2,256]{1,0:T(2,128)}, u32[]{:S(2)}) copy-start(f32[2,256]{1,0:T(2,128)} %get-tuple-element.366) | copy-start | bytes 6148
  81.9 28.0 %copy-start.8 = (f32[2,128,128]{2,1,0:T(8,128)}, f32[2,128,128]{2,1,0:T(8,128)S(1)}, u32[]{:S(2)}) copy-start(f32[2,128,128]{2,1,0:T(8,128)S(1)} %collective-permute-done.6) | copy-start | bytes 393220
  81.9 7.2 %collective-permute-start.7 = (f32[2,128,128]{2,1,0:T(8,128)S(1)}, f32[2,128,128]{2,1,0:T(8,128)S(1)}, u32[]{:S(2)}, u32[]{:S(2)}) collective-permute-start(f32[2,128,128]{2,1,0:T(8,128)S(1)} %add.290), channel_id=1, source_target_pairs={{0,64},{8,72},{16,80},{24,88},{32,96},{40,104},{48,112},{56,120},{... | collective-permute-start | bytes 393224 | tf_op jit(solution)/shard_map/ppermute | solution.py:29
  89.1 24.9 %copy-start.10 = (f32[2,128,128]{2,1,0:T(8,128)}, f32[2,128,128]{2,1,0:T(8,128)S(1)}, u32[]{:S(2)}) copy-start(f32[2,128,128]{2,1,0:T(8,128)S(1)} %collective-permute-done.7) | copy-start | bytes 393220
  89.1 11.0 %collective-permute-start.8 = (f32[2,128,128]{2,1,0:T(8,128)S(1)}, f32[2,128,128]{2,1,0:T(8,128)S(1)}, u32[]{:S(2)}, u32[]{:S(2)}) collective-permute-start(f32[2,128,128]{2,1,0:T(8,128)S(1)} %add.292), channel_id=1, source_target_pairs={{0,128},{8,136},{16,144},{24,152},{32,160},{40,168},{48,176},{56,1... | collective-permute-start | bytes 393224 | tf_op jit(solution)/shard_map/ppermute | solution.py:29
  100.2 13.8 %copy-start.12 = (f32[2,128,128]{2,1,0:T(8,128)}, f32[2,128,128]{2,1,0:T(8,128)S(1)}, u32[]{:S(2)}) copy-start(f32[2,128,128]{2,1,0:T(8,128)S(1)} %collective-permute-done.8) | copy-start | bytes 393220
  100.2 13.8 %collective-permute-start.9 = (f32[2,128,128]{2,1,0:T(8,128)S(1)}, f32[2,128,128]{2,1,0:T(8,128)S(1)}, u32[]{:S(2)}, u32[]{:S(2)}) collective-permute-start(f32[2,128,128]{2,1,0:T(8,128)S(1)} %add.294), channel_id=1, source_target_pairs={{0,256},{8,264},{16,272},{24,280},{32,288},{40,296},{48,304},{56,3... | collective-permute-start | bytes 393224 | tf_op jit(solution)/shard_map/ppermute | solution.py:29
  116.0 26.4 %copy-start.4 = (f32[2,256,128]{1,2,0:T(8,128)}, f32[2,256,128]{1,2,0:T(8,128)S(1)}, u32[]{:S(2)}) copy-start(f32[2,256,128]{1,2,0:T(8,128)S(1)} %get-tuple-element.344) | copy-start | bytes 786436
  116.6 9.7 %all-to-all-start = ((f32[8,1,256]{2,1,0:T(1,128)}), f32[8,1,256]{2,1,0:T(1,128)}, u32[]{:S(2)}, u32[]{:S(2)}) async-start(f32[8,1,256]{2,1,0:T(1,128)} %broadcast_in_dim.80), calls=%async_computation | async-start | bytes 16384 | tf_op jit(solution)/shard_map/all_to_all | solution.py:34
  131.1 9.3 %all-to-all-start.1 = ((f32[8,1,256]{2,1,0:T(1,128)}), f32[8,1,256]{2,1,0:T(1,128)}, u32[]{:S(2)}, u32[]{:S(2)}) async-start(f32[8,1,256]{2,1,0:T(1,128)} %broadcast_in_dim.81), calls=%async_computation.1 | async-start | bytes 16384 | tf_op jit(solution)/shard_map/all_to_all | solution.py:34
  142.4 2.8 copy-start.41
  146.1 3.4 %copy-start.17 = (bf16[2,2,128,128]{3,2,1,0:T(8,128)(2,1)S(1)}, bf16[2,2,128,128]{3,2,1,0:T(8,128)(2,1)}, u32[]{:S(2)}) copy-start(bf16[2,2,128,128]{3,2,1,0:T(8,128)(2,1)} %copy-done.16) | copy-start | bytes 393220
  148.8 7.9 %copy-start.5 = (f32[2,1280,128]{1,2,0:T(8,128)S(1)}, f32[2,1280,128]{1,2,0:T(8,128)}, u32[]{:S(2)}) copy-start(f32[2,1280,128]{1,2,0:T(8,128)} %custom-call.6) | copy-start | bytes 3932164
  149.6 5.2 %copy-start.34 = (bf16[2,256,128]{2,1,0:T(8,128)(2,1)S(1)}, bf16[2,256,128]{2,1,0:T(8,128)(2,1)}, u32[]{:S(2)}) copy-start(bf16[2,256,128]{2,1,0:T(8,128)(2,1)} %copy-done.33) | copy-start | bytes 393220
  149.6 5.2 %copy-start.36 = (bf16[2,4,64,64]{3,2,1,0:T(8,128)(2,1)S(1)}, bf16[2,4,64,64]{3,2,1,0:T(8,128)(2,1)}, u32[]{:S(2)}) copy-start(bf16[2,4,64,64]{3,2,1,0:T(8,128)(2,1)} %copy-done.35) | copy-start | bytes 196612
  173.0 12.8 %copy-start.6 = (f32[2,1280,128]{1,2,0:T(8,128)}, f32[2,1280,128]{1,2,0:T(8,128)S(1)}, u32[]{:S(2)}) copy-start(f32[2,1280,128]{1,2,0:T(8,128)S(1)} %get-tuple-element.227) | copy-start | bytes 3932164
  180.1 5.6 %copy-start.7 = (f32[2,1280,128]{1,2,0:T(8,128)S(1)}, f32[2,1280,128]{1,2,0:T(8,128)}, u32[]{:S(2)}) copy-start(f32[2,1280,128]{1,2,0:T(8,128)} %get-tuple-element.228) | copy-start | bytes 3932164
  182.9 73.8 %collective-permute-start.10 = (bf16[6,2,128,128]{2,3,1,0:T(8,128)(2,1)}, bf16[6,2,128,128]{2,3,1,0:T(8,128)(2,1)}, u32[]{:S(2)}, u32[]{:S(2)}) collective-permute-start(bf16[6,2,128,128]{2,3,1,0:T(8,128)(2,1)} %fusion.119), channel_id=1, source_target_pairs={{0,8},{8,0},{16,24},{24,16},{32,40},{40,32},{48,56},{56,48},{64,72... | collective-permute-start | bytes 1179656 | tf_op jit(solution)/shard_map/ppermute | solution.py:29
  186.0 17.0 %copy-start.32 = (f32[2,1,1,128,128]{4,3,0,2,1:T(8,128)S(1)}, f32[2,1,1,128,128]{4,3,0,2,1:T(8,128)}, u32[]{:S(2)}) copy-start(f32[2,1,1,128,128]{4,3,0,2,1:T(8,128)} %convolution_bitcast_fusion.25) | copy-start | bytes 393220
  186.8 65.7 %collective-permute-start.19 = (bf16[2,2,256,128]{2,3,1,0:T(8,128)(2,1)}, bf16[2,2,256,128]{2,3,1,0:T(8,128)(2,1)}, u32[]{:S(2)}, u32[]{:S(2)}) collective-permute-start(bf16[2,2,256,128]{2,3,1,0:T(8,128)(2,1)} %pad_maximum_fusion.4), channel_id=1, source_target_pairs={{32,0},{40,8},{48,16},{56,24},{64,32},{72,40},{80,48},{88,56},{96,... | collective-permute-start | bytes 786440 | tf_op jit(solution)/shard_map/ppermute | solution.py:25
  193.6 59.8 %collective-permute-start.18 = (bf16[2,2,256,128]{2,3,1,0:T(8,128)(2,1)}, bf16[2,2,256,128]{2,3,1,0:T(8,128)(2,1)}, u32[]{:S(2)}, u32[]{:S(2)}) collective-permute-start(bf16[2,2,256,128]{2,3,1,0:T(8,128)(2,1)} %pad_maximum_fusion.3), channel_id=1, source_target_pairs={{24,0},{32,8},{40,16},{48,24},{56,32},{64,40},{72,48},{80,56},{88,... | collective-permute-start | bytes 786440 | tf_op jit(solution)/shard_map/ppermute | solution.py:25
  196.6 8.4 %copy-start.59 = (f32[2,256]{1,0:T(2,128)S(1)}, f32[2,256]{1,0:T(2,128)}, u32[]{:S(2)}) copy-start(f32[2,256]{1,0:T(2,128)} %get-tuple-element.299) | copy-start | bytes 6148
  196.6 8.4 %copy-start.58 = (f32[2,256]{1,0:T(2,128)S(1)}, f32[2,256]{1,0:T(2,128)}, u32[]{:S(2)}) copy-start(f32[2,256]{1,0:T(2,128)} %get-tuple-element.298) | copy-start | bytes 6148
  196.7 8.4 %copy-start.57 = (f32[2,256]{1,0:T(2,128)S(1)}, f32[2,256]{1,0:T(2,128)}, u32[]{:S(2)}) copy-start(f32[2,256]{1,0:T(2,128)} %get-tuple-element.297) | copy-start | bytes 6148
  196.7 8.4 %copy-start.56 = (f32[2,256]{1,0:T(2,128)S(1)}, f32[2,256]{1,0:T(2,128)}, u32[]{:S(2)}) copy-start(f32[2,256]{1,0:T(2,128)} %get-tuple-element.296) | copy-start | bytes 6148
  196.7 8.4 %copy-start.55 = (f32[2,256]{1,0:T(2,128)S(1)}, f32[2,256]{1,0:T(2,128)}, u32[]{:S(2)}) copy-start(f32[2,256]{1,0:T(2,128)} %get-tuple-element.295) | copy-start | bytes 6148
  196.7 8.4 %copy-start.51 = (f32[2,256]{1,0:T(2,128)S(1)}, f32[2,256]{1,0:T(2,128)}, u32[]{:S(2)}) copy-start(f32[2,256]{1,0:T(2,128)} %get-tuple-element.291) | copy-start | bytes 6148
  196.7 8.4 %copy-start.52 = (f32[2,256]{1,0:T(2,128)S(1)}, f32[2,256]{1,0:T(2,128)}, u32[]{:S(2)}) copy-start(f32[2,256]{1,0:T(2,128)} %get-tuple-element.292) | copy-start | bytes 6148
  196.7 8.4 %copy-start.53 = (f32[2,256]{1,0:T(2,128)S(1)}, f32[2,256]{1,0:T(2,128)}, u32[]{:S(2)}) copy-start(f32[2,256]{1,0:T(2,128)} %get-tuple-element.293) | copy-start | bytes 6148
  196.7 8.4 %copy-start.54 = (f32[2,256]{1,0:T(2,128)S(1)}, f32[2,256]{1,0:T(2,128)}, u32[]{:S(2)}) copy-start(f32[2,256]{1,0:T(2,128)} %get-tuple-element.294) | copy-start | bytes 6148
  196.7 8.4 %copy-start.61 = (s32[256,6]{0,1:T(8,128)S(1)}, s32[256,6]{0,1:T(8,128)}, u32[]{:S(2)}) copy-start(s32[256,6]{0,1:T(8,128)} %param.25) | copy-start | bytes 18436
  196.7 8.6 %copy-start.18 = (f32[2,4,64,128]{3,2,1,0:T(8,128)S(1)}, f32[2,4,64,128]{3,2,1,0:T(8,128)}, u32[]{:S(2)}) copy-start(f32[2,4,64,128]{3,2,1,0:T(8,128)} %fusion.203) | copy-start | bytes 786436
  196.7 8.6 %copy-start.22 = (f32[2,1,2,128,128]{4,3,2,0,1:T(8,128)S(1)}, f32[2,1,2,128,128]{4,3,2,0,1:T(8,128)}, u32[]{:S(2)}) copy-start(f32[2,1,2,128,128]{4,3,2,0,1:T(8,128)} %stack.159.clone) | copy-start | bytes 786436
  196.8 8.6 %copy-start.24 = (f32[2,2,2,64,128]{4,3,2,1,0:T(8,128)S(1)}, f32[2,2,2,64,128]{4,3,2,1,0:T(8,128)}, u32[]{:S(2)}) copy-start(f32[2,2,2,64,128]{4,3,2,1,0:T(8,128)} %stack.157.clone) | copy-start | bytes 786436
  197.5 57.0 %collective-permute-start.17 = (bf16[2,2,256,128]{2,3,1,0:T(8,128)(2,1)}, bf16[2,2,256,128]{2,3,1,0:T(8,128)(2,1)}, u32[]{:S(2)}, u32[]{:S(2)}) collective-permute-start(bf16[2,2,256,128]{2,3,1,0:T(8,128)(2,1)} %pad_maximum_fusion.2), channel_id=1, source_target_pairs={{16,0},{24,8},{32,16},{40,24},{48,32},{56,40},{64,48},{72,56},{80,... | collective-permute-start | bytes 786440 | tf_op jit(solution)/shard_map/ppermute | solution.py:25
  200.4 55.1 %collective-permute-start.16 = (bf16[2,2,256,128]{2,3,1,0:T(8,128)(2,1)}, bf16[2,2,256,128]{2,3,1,0:T(8,128)(2,1)}, u32[]{:S(2)}, u32[]{:S(2)}) collective-permute-start(bf16[2,2,256,128]{2,3,1,0:T(8,128)(2,1)} %pad_maximum_fusion.1), channel_id=1, source_target_pairs={{8,0},{16,8},{24,16},{32,24},{40,32},{48,40},{56,48},{64,56},{72,6... | collective-permute-start | bytes 786440 | tf_op jit(solution)/shard_map/ppermute | solution.py:25
  206.2 45.3 %copy-start.39 = (f32[2,256,128]{2,1,0:T(8,128)S(1)}, f32[2,256,128]{2,1,0:T(8,128)}, u32[]{:S(2)}) copy-start(f32[2,256,128]{2,1,0:T(8,128)} %get-tuple-element.226) | copy-start | bytes 786436
  253.5 3.2 copy-start.27
  255.5 6.9 %copy-start.19 = (f32[2,256,128]{1,2,0:T(8,128)S(1)}, f32[2,256,128]{1,2,0:T(8,128)}, u32[]{:S(2)}) copy-start(f32[2,256,128]{1,2,0:T(8,128)} %copy.222) | copy-start | bytes 786436
  255.5 6.9 %copy-start.20 = (f32[2,256,128]{1,2,0:T(8,128)S(1)}, f32[2,256,128]{1,2,0:T(8,128)}, u32[]{:S(2)}) copy-start(f32[2,256,128]{1,2,0:T(8,128)} %copy.218) | copy-start | bytes 786436
  256.6 6.9 %copy-start.21 = (f32[2,256,128]{1,2,0:T(8,128)S(1)}, f32[2,256,128]{1,2,0:T(8,128)}, u32[]{:S(2)}) copy-start(f32[2,256,128]{1,2,0:T(8,128)} %reshape.296) | copy-start | bytes 786436
  256.6 6.9 %copy-start.23 = (f32[2,256,128]{1,2,0:T(8,128)S(1)}, f32[2,256,128]{1,2,0:T(8,128)}, u32[]{:S(2)}) copy-start(f32[2,256,128]{1,2,0:T(8,128)} %copy.234) | copy-start | bytes 786436
  256.6 6.9 %copy-start.25 = (f32[2,256,128]{1,2,0:T(8,128)S(1)}, f32[2,256,128]{1,2,0:T(8,128)}, u32[]{:S(2)}) copy-start(f32[2,256,128]{1,2,0:T(8,128)} %copy.235) | copy-start | bytes 786436
  257.8 15.8 %collective-permute-start.11 = (bf16[5,2,128,128]{2,3,1,0:T(8,128)(2,1)S(1)}, bf16[5,2,128,128]{2,3,1,0:T(8,128)(2,1)S(1)}, u32[]{:S(2)}, u32[]{:S(2)}) collective-permute-start(bf16[5,2,128,128]{2,3,1,0:T(8,128)(2,1)S(1)} %get-tuple-element.341), channel_id=1, source_target_pairs={{0,16},{8,24},{16,0},{24,8},{32,48},{40,56},{48,32},{56,40},{64,80... | collective-permute-start | bytes 983048 | tf_op jit(solution)/shard_map/ppermute | solution.py:29
  273.7 18.4 %collective-permute-start.12 = (bf16[4,2,128,128]{2,3,1,0:T(8,128)(2,1)S(1)}, bf16[4,2,128,128]{2,3,1,0:T(8,128)(2,1)S(1)}, u32[]{:S(2)}, u32[]{:S(2)}) collective-permute-start(bf16[4,2,128,128]{2,3,1,0:T(8,128)(2,1)S(1)} %get-tuple-element.339), channel_id=1, source_target_pairs={{0,32},{8,40},{16,48},{24,56},{32,0},{40,8},{48,16},{56,24},{64,96... | collective-permute-start | bytes 786440 | tf_op jit(solution)/shard_map/ppermute | solution.py:29
  292.2 8.7 %collective-permute-start.13 = (bf16[3,2,128,128]{2,3,1,0:T(8,128)(2,1)S(1)}, bf16[3,2,128,128]{2,3,1,0:T(8,128)(2,1)S(1)}, u32[]{:S(2)}, u32[]{:S(2)}) collective-permute-start(bf16[3,2,128,128]{2,3,1,0:T(8,128)(2,1)S(1)} %get-tuple-element.337), channel_id=1, source_target_pairs={{0,64},{8,72},{16,80},{24,88},{32,96},{40,104},{48,112},{56,120},{... | collective-permute-start | bytes 589832 | tf_op jit(solution)/shard_map/ppermute | solution.py:29
  301.0 10.2 %collective-permute-start.14 = (bf16[2,2,128,128]{2,3,1,0:T(8,128)(2,1)S(1)}, bf16[2,2,128,128]{2,3,1,0:T(8,128)(2,1)S(1)}, u32[]{:S(2)}, u32[]{:S(2)}) collective-permute-start(bf16[2,2,128,128]{2,3,1,0:T(8,128)(2,1)S(1)} %get-tuple-element.335), channel_id=1, source_target_pairs={{0,128},{8,136},{16,144},{24,152},{32,160},{40,168},{48,176},{56,1... | collective-permute-start | bytes 393224 | tf_op jit(solution)/shard_map/ppermute | solution.py:29
  311.2 10.2 %collective-permute-start.15 = (bf16[1,2,128,128]{2,3,1,0:T(8,128)(2,1)S(1)}, bf16[1,2,128,128]{2,3,1,0:T(8,128)(2,1)S(1)}, u32[]{:S(2)}, u32[]{:S(2)}) collective-permute-start(bf16[1,2,128,128]{2,3,1,0:T(8,128)(2,1)S(1)} %fusion.115), channel_id=1, source_target_pairs={{0,256},{8,264},{16,272},{24,280},{32,288},{40,296},{48,304},{56,3... | collective-permute-start | bytes 196616 | tf_op jit(solution)/shard_map/ppermute | solution.py:29
  (25 other events, 41.9 us)
where the time goes:
time: 330 us; the launch traced here: 325 us
  waiting for transfers between devices  93.1 us (28%)
  starting transfers between devices  92.1 us (28%)
  blocking collectives  43.7 us (13%)
  matrix products  43.6 us (13%)
  local copies, waits for them, and re-layouts  26.9 us (8%)
  other arithmetic  20.8 us (6%)
    ppermute x12, waiting for transfers between devices, from_partner(): lax.ppermute(shard, axis, [(i, i ^ 1 << bit) for i in range(lax.axis_size...  84.1 us
    ppermute x12, starting transfers between devices, from_partner(): lax.ppermute(shard, axis, [(i, i ^ 1 << bit) for i in range(lax.axis_size...  51.5 us
    psum x2, blocking collectives, over_axes(): return functools.reduce(lax.psum, axes, shard)  43.7 us
    dot_general x56, matrix products, contract(): jnp.einsum(pattern, left_side, right_side, preferred_element_type=jnp.flo...  42.6 us
    ppermute x8, starting transfers between devices, shifted(): return lax.ppermute(block, axis, route)  32.4 us
    unnamed x138, local copies, waits for them, and re-layouts  9.13 us
    all_to_all x2, waiting for transfers between devices, copy_for_each(): return lax.all_to_all(copies, axis, split_axis=0, concat_axis=0, tiled=True)  9 us
    all_to_all x2, starting transfers between devices, copy_for_each(): return lax.all_to_all(copies, axis, split_axis=0, concat_axis=0, tiled=True)  8.24 us
  transfers between devices with their start and end apart: 22, of which 12 were waited for; matrix products, arithmetic and copies ran while one was open for 11% of the time, Pallas kernels for 0%

commit v1 on v0

v1 whole, which is shorter than its diff:
```python
import functools
import math

import jax
import jax.numpy as jnp
from jax import lax
from jax.experimental import pallas as pl
from jax.experimental.pallas import tpu as pltpu
from jax.sharding import Mesh
from jax.sharding import PartitionSpec as P

BLOCK = 64
LEVELS = 6
ROWS = 16
REACH = 4
HEADS = 2
T = 256
D = 128
RING = 8
PIECE = D // RING
EPS = 1e-06
BF = jnp.bfloat16
F32 = jnp.float32
HIGH = lax.Precision.HIGHEST
MESH = pl.DeviceIdType.MESH


def level_scale(group_len):
    return 1.0 / math.sqrt(group_len * D)


def nn(a, b):
    return lax.dot_general(a, b, (((1,), (0,)), ((), ())), preferred_element_type=F32)


def nt(a, b, precision=None):
    return lax.dot_general(
        a, b, (((1,), (1,)), ((), ())), precision=precision, preferred_element_type=F32
    )


def tn(a, b, precision=None):
    return lax.dot_general(
        a, b, (((0,), (0,)), ((), ())), precision=precision, preferred_element_type=F32
    )


def iota(shape, dim):
    return lax.broadcasted_iota(jnp.int32, shape, dim)


def kernel(
    dims,
    q_in,
    k_in,
    v_in,
    g_in,
    gain,
    table,
    index,
    window,
    out,
    dq_out,
    dk_out,
    dv_out,
    table_out,
    gain_out,
    own,
    kv,
    qs,
    ds,
    ws,
    w_own,
    w_wide,
    w_far,
    p_raw,
    a_mix,
    p_low,
    p_far,
    s_near,
    mix,
    dm,
    rs_send,
    rs_recv,
    z_send,
    z_recv,
    ag_send,
    ag_recv,
    n_send,
    n_recv,
    r_send,
    r_recv,
    in_sem,
    kv_ss,
    kv_rs,
    q_ss,
    q_rs,
    d_ss,
    d_rs,
    w_ss,
    w_rs,
    f_ss,
    f_rs,
    n_ss,
    n_rs,
    r_ss,
    r_rs,
):
    nz, ny, nh = dims
    z = lax.axis_index("seq_0")
    y = lax.axis_index("seq_1")
    hd = lax.axis_index("head")
    s = z * ny + y
    shard_count = nz * ny

    def y_peer(d):
        return (z, lax.rem(y + d, ny), hd)

    def z_peer(d):
        return (lax.rem(z + d, nz), y, hd)

    def h_peer(d):
        return (z, y, lax.rem(hd + d, nh))

    def s_peer(d):
        to = lax.rem(s + d + shard_count, shard_count)
        return (lax.div(to, ny), lax.rem(to, ny), hd)

    def remote(src, dst, ss, rs, to):
        return pltpu.make_async_remote_copy(
            src_ref=src, dst_ref=dst, send_sem=ss, recv_sem=rs, device_id=to, device_id_type=MESH
        )

    sent = []

    def go(copy):
        copy.start()
        sent.append(copy)
        return copy

    barrier = pltpu.get_barrier_semaphore()
    peers = [s_peer(1), s_peer(-1)]
    peers += [y_peer(d) for d in range(1, ny)]
    peers += [z_peer(d) for d in range(1, nz)]
    peers += [h_peer(d) for d in range(1, nh)]
    for peer in peers:
        pl.semaphore_signal(barrier, inc=1, device_id=peer, device_id_type=MESH)

    loads = []
    for n, ref in enumerate((k_in, v_in, q_in, g_in)):
        load = pltpu.make_async_copy(ref, own.at[n], in_sem.at[n])
        load.start()
        loads.append(load)
    loads[0].wait()
    loads[1].wait()
    K, V, Q, G = 0, 1, 2, 3

    for h in range(HEADS):
        state = tn(own[K, h], own[V, h])
        rs_send[0, :, h] = state.astype(BF).reshape(RING, PIECE, D)

    pl.semaphore_wait(barrier, len(peers))

    def scatter_start(side):
        copies = []
        for d in range(1, ny):
            to = lax.rem(y + d, ny)
            copies.append(
                go(
                    remote(
                        rs_send.at[side, to],
                        rs_recv.at[side, y],
                        f_ss.at[side, 0, d],
                        f_rs.at[side, 0, d],
                        y_peer(d),
                    )
                )
            )
        rs_recv[side, pl.ds(y, 1)] = rs_send[side, pl.ds(y, 1)]
        return copies

    def across_start(side, scattered):
        for copy in scattered:
            copy.wait_recv()
        half = RING // 2
        pieces = [rs_recv[side, n].astype(F32) for n in range(RING)]
        low = functools.reduce(jnp.add, pieces[:half])
        upper = functools.reduce(jnp.add, pieces[half:])
        z_send[side] = (low + upper).astype(BF)
        copies = []
        for d in range(1, nz):
            copies.append(
                go(
                    remote(
                        z_send.at[side],
                        z_recv.at[side, d],
                        f_ss.at[side, 1, d],
                        f_rs.at[side, 1, d],
                        z_peer(d),
                    )
                )
            )
        return copies, (low if side == 0 else upper)

    def gather_start(side, across, near):
        total = jnp.zeros((HEADS, PIECE, D), F32)
        for d in range(1, nz):
            across[d - 1].wait_recv()
            other = lax.rem(z - d + nz, nz)
            counts = (other < z) if side == 0 else (other > z)
            scale = jnp.where(
                lax.div(other, 2) == lax.div(z, 2),
                level_scale(T * 8),
                jnp.where(
                    lax.div(other, 4) == lax.div(z, 4), level_scale(T * 16), level_scale(T * 32)
                ),
            )
            scale = jnp.where(counts, scale, 0.0)
            total = total + z_recv[side, d].astype(F32) * scale
        with_near = (total + near * level_scale(T * 4)).astype(BF)
        plain = total.astype(BF)
        ag_send[side, 0] = plain if side == 0 else with_near
        ag_send[side, 1] = with_near if side == 0 else plain
        copies = []
        for d in range(1, ny):
            to = lax.rem(y + d, ny)
            copies.append(
                go(
                    remote(
                        ag_send.at[side, lax.div(to, RING // 2)],
                        ag_recv.at[side, y],
                        f_ss.at[side, 2, d],
                        f_rs.at[side, 2, d],
                        y_peer(d),
                    )
                )
            )
        ag_recv[side, pl.ds(y, 1)] = ag_send[side, pl.ds(lax.div(y, RING // 2), 1)]
        return copies

    def gathered(side, h):
        return ag_recv[side, :, h].reshape(D, D)

    def kv_hop(j, c):
        src = (k_in, v_in)[c] if j == 1 else kv.at[j - 2, c]
        return go(remote(src, kv.at[j - 1, c], kv_ss.at[j - 1, c], kv_rs.at[j - 1, c], s_peer(1)))

    def q_hop(j):
        src = q_in if j == 1 else qs.at[j - 2]
        return go(remote(src, qs.at[j - 1], q_ss.at[j - 1], q_rs.at[j - 1], s_peer(-1)))

    def w_hop(j):
        src = w_own if j == 1 else ws.at[j - 2]
        return go(remote(src, ws.at[j - 1], w_ss.at[j - 1], w_rs.at[j - 1], s_peer(-1)))

    def d_hop(j, h):
        src = dm.at[h] if j == 1 else ds.at[j - 2, h]
        return go(
            remote(src, ds.at[j - 1, h], d_ss.at[j - 1, h], d_rs.at[j - 1, h], s_peer(-1))
        )

    scattered = scatter_start(0)
    kv_now = [kv_hop(1, K), kv_hop(1, V)]
    q_now = q_hop(1)

    index_row = index[...]
    for h in range(HEADS):
        rows = []
        for j in range(LEVELS):
            picked = index_row[j : j + 1]
            row = jnp.zeros((1, T), F32)
            for k in range(ROWS):
                row = jnp.where(picked == k, table[j, h, k], row)
            rows.append(row)
        rows.append(jnp.zeros((8 - LEVELS, T), F32))
        w_own[8 * h : 8 * h + 8] = jnp.concatenate(rows, axis=0)
    w_now = w_hop(1)
    spread = []
    for h in range(HEADS):
        for j in range(LEVELS):
            spread.append((iota((16, D), 0) == 8 * h + j).astype(F32))
    w_wide[...] = tn(w_own[...], jnp.concatenate(spread, axis=1), HIGH)

    def weight(h, j):
        at = (h * LEVELS + j) * D
        return w_wide[:, at : at + D]

    def window_scale(h, lanes):
        return lax.rsqrt(jnp.full((1, lanes), D * window[h], jnp.int32).astype(F32))

    token = iota((T, T), 0)
    key = iota((T, T), 1)
    pair_gap = token - key
    token_block = token >> 6
    key_block = key >> 6
    causal = pair_gap >= 0
    same_leaf = token_block == key_block
    same_pair = (token_block >> 1) == (key_block >> 1)

    def twice(half):
        return jnp.concatenate([half, half], axis=1)

    loads[2].wait()
    loads[3].wait()
    for h in range(HEADS):
        raw = nt(own[Q, h], own[K, h])
        scale0 = twice(weight(h, 0) * level_scale(BLOCK))
        scale1 = twice(weight(h, 1) * level_scale(BLOCK))
        scale2 = twice(weight(h, 2) * level_scale(2 * BLOCK))
        scale = jnp.where(same_leaf, scale0, jnp.where(same_pair, scale1, scale2))
        scale = jnp.where(causal, scale + window_scale(h, T), 0.0)
        low = (raw * scale).astype(BF)
        p_raw[h] = raw
        a_mix[h] = scale
        p_low[h] = low
        mix[h] = nn(low, own[V, h])

    def reach_q(h, j):
        limit = jnp.where(s >= j, window[h] - T * j, -T * (REACH + 1))
        return pair_gap < limit

    def reach_k(h, j):
        limit = jnp.where(s + j < shard_count, window[h] - T * j, -T * (REACH + 1))
        return -pair_gap < limit

    def far_probs(j):
        for h in range(HEADS):
            score = nt(own[K, h], qs[j - 1, h])
            p_far[j - 2, h] = jnp.where(reach_k(h, j), score, 0.0).astype(BF)

    def far_weights(j):
        spread = []
        for h in range(HEADS):
            for n in (3, 4):
                spread.append((iota((16, D), 0) == 8 * h + n).astype(F32))
        w_far[j - 1] = tn(ws[j - 1], jnp.concatenate(spread, axis=1), HIGH)

    odd = lax.rem(s, 2)
    odd_f = odd.astype(F32)
    second_f = lax.rem(lax.div(s, 2), 2).astype(F32)
    any_before = (s >= 1).astype(F32)
    any_after = (s + 1 < shard_count).astype(F32)

    def near_scale(h, wide):
        return window_scale(h, D) * any_before + wide * (odd_f * level_scale(T))

    def window_part(h, j):
        score = nt(own[Q, h], kv[j - 1, K, h])
        prob = jnp.where(reach_q(h, j), score, 0.0).astype(BF)
        return nn(prob, kv[j - 1, V, h]) * window_scale(h, D)

    q_now.wait_recv()
    q_now = q_hop(2)
    w_now.wait_recv()
    w_now = w_hop(2)
    far_weights(1)

    across, near = across_start(0, scattered)

    kv_now[K].wait_recv()
    kv_next = [kv_hop(2, K)]
    kv_now[V].wait_recv()
    kv_next.append(kv_hop(2, V))
    kv_now = kv_next
    for h in range(HEADS):
        state = tn(kv[0, K, h], kv[0, V, h]).astype(BF)
        s_near[0, h] = state
        mix[h] = mix[h] + near_scale(h, weight(h, 3)) * nn(own[Q, h], state)

    q_now.wait_recv()
    q_now = q_hop(3)
    w_now.wait_recv()
    w_now = w_hop(3)
    far_weights(2)
    far_probs(2)

    gather = gather_start(0, across, near)

    kv_now[K].wait_recv()
    kv_next = [kv_hop(3, K)]
    kv_now[V].wait_recv()
    kv_next.append(kv_hop(3, V))
    kv_now = kv_next
    for h in range(HEADS):
        mix[h] = mix[h] + window_part(h, 2)

    q_now.wait_recv()
    q_now = q_hop(4)
    w_now.wait_recv()
    far_weights(3)
    far_probs(3)

    for copy in gather:
        copy.wait_recv()
    for h in range(HEADS):
        mix[h] = mix[h] + weight(h, 5) * nn(own[Q, h], gathered(0, h))

    kv_now[K].wait_recv()
    kv_next = [kv_hop(4, K)]
    kv_now[V].wait_recv()
    kv_next.append(kv_hop(4, V))
    kv_now = kv_next
    for h in range(HEADS):
        state = tn(kv[odd, K, h], kv[odd, V, h]) + tn(kv[odd + 1, K, h], kv[odd + 1, V, h])
        state = (state * (second_f * level_scale(2 * T))).astype(BF)
        s_near[1, h] = state
        mix[h] = mix[h] + window_part(h, 3) + weight(h, 4) * nn(own[Q, h], state)

    q_now.wait_recv()
    far_probs(4)

    kv_now[K].wait_recv()
    kv_now[V].wait_recv()
    square = jnp.zeros((T, D), F32)
    cross = jnp.zeros((T, D), F32)
    for h in range(HEADS):
        mixed = mix[h] + window_part(h, 4)
        mix[h] = mixed
        square = square + mixed * mixed
        cross = cross + own[G, h].astype(F32) * gain[h : h + 1] * mixed

    both = jnp.concatenate([square, cross], axis=1)
    pick = (iota((8, 2 * D), 0) == (iota((8, 2 * D), 1) >> 7)).astype(F32)
    n_send[...] = nt(pick, both, HIGH)
    norms = []
    for d in range(1, nh):
        norms.append(go(remote(n_send, n_recv.at[hd], n_ss.at[d], n_rs.at[d], h_peer(d))))
    n_recv[pl.ds(hd, 1)] = n_send[...][None]
    for copy in norms:
        copy.wait_recv()
    sums = functools.reduce(jnp.add, [n_recv[n] for n in range(nh)])
    inv_row = lax.rsqrt(sums[0:1] * (1.0 / (HEADS * nh * D)) + EPS)
    back_row = inv_row * inv_row * inv_row * sums[1:2] * (1.0 / (HEADS * nh * D))
    both_rows = jnp.concatenate([inv_row, back_row, jnp.zeros((6, T), F32)], axis=0)
    wide = tn(both_rows, pick, HIGH)
    inv_rms = wide[:, :D]
    back = wide[:, D:]

    d_now = []
    grads = []
    for h in range(HEADS):
        given = own[G, h].astype(F32)
        grad = given * gain[h : h + 1] * inv_rms - mix[h] * back
        dm[h] = grad.astype(BF)
        grads.append(grad)
        d_now.append(d_hop(1, h))
    for h in range(HEADS):
        up = (weight(h, 5) * grads[h]).astype(BF)
        state = tn(own[Q, h], up)
        rs_send[1, :, h] = state.astype(BF).reshape(RING, PIECE, D)
    scattered = scatter_start(1)

    gain_rows = []
    for h in range(HEADS):
        scaled = mix[h] * inv_rms
        out[h] = (scaled * gain[h : h + 1]).astype(BF)
        gain_rows.append(jnp.sum(own[G, h].astype(F32) * scaled, axis=0, keepdims=True))

    lane_block = iota((8, T), 1) >> 6
    row_no = iota((8, T), 0)
    hot = jnp.concatenate(
        [(index_row[j : j + 1] == iota((ROWS, T), 0)).astype(F32) for j in range(LEVELS)], axis=0
    )
    dq = []
    dk = []
    dv = []
    for h in range(HEADS):
        grad = grads[h]
        low = dm[h]
        prob_grad = nt(low, own[V, h])
        product = jnp.where(causal, p_raw[h] * prob_grad, 0.0)
        score_grad = (prob_grad * a_mix[h]).astype(BF)
        dk.append(tn(score_grad, own[Q, h]))
        dv.append(tn(p_low[h], low))
        up1 = (near_scale(h, weight(h, 3)) * grad).astype(BF)
        up4 = (weight(h, 4) * grad).astype(BF)
        up5 = (weight(h, 5) * grad).astype(BF)
        dq.append(
            nn(score_grad, own[K, h])
            + nt(up1, s_near[0, h])
            + nt(up4, s_near[1, h])
            + nt(up5, gathered(0, h))
        )
        by_block = nt((row_no == lane_block).astype(F32), product, HIGH)
        row0 = jnp.sum(jnp.where(row_no == lane_block, by_block, 0.0), axis=0, keepdims=True)
        row1 = jnp.sum(
            jnp.where((row_no == lane_block - 1) & ((lane_block & 1) == 1), by_block, 0.0),
            axis=0,
            keepdims=True,
        )
        row2 = jnp.sum(
            jnp.where((row_no < 2) & (lane_block >= 2), by_block, 0.0), axis=0, keepdims=True
        )
        areas = jnp.concatenate(
            [
                grad * nn(own[Q, h], s_near[0, h]) * (odd_f * level_scale(T)),
                grad * nn(own[Q, h], s_near[1, h]),
                grad * nn(own[Q, h], gathered(0, h)),
            ],
            axis=1,
        )
        pick3 = (iota((8, 3 * D), 0) == (iota((8, 3 * D), 1) >> 7)).astype(F32)
        far_rows = nt(pick3, areas, HIGH)
        weight_rows = jnp.concatenate(
            [
                row0 * level_scale(BLOCK),
                row1 * level_scale(BLOCK),
                row2 * level_scale(2 * BLOCK),
                far_rows[0:3],
                jnp.zeros((2, T), F32),
            ],
            axis=0,
        )
        by_level = nt(weight_rows, hot, HIGH)
        part = jnp.zeros((8, ROWS), F32)
        for j in range(LEVELS):
            slab = by_level[:, ROWS * j : ROWS * (j + 1)]
            part = part + jnp.where(iota((8, ROWS), 0) == j, slab, 0.0)
        r_send[0, 8 * h : 8 * h + 8] = jnp.concatenate(
            [part, jnp.zeros((8, D - ROWS), F32)], axis=1
        )

    r_send[0, 16:24] = jnp.concatenate(gain_rows + [jnp.zeros((6, D), F32)], axis=0)

    def reduce_start(step):
        count, me, peer = ((ny, y, y_peer), (nz, z, z_peer))[step]
        copies = []
        for d in range(1, count):
            copies.append(
                go(
                    remote(
                        r_send.at[step],
                        r_recv.at[step, me],
                        r_ss.at[step, d],
                        r_rs.at[step, d],
                        peer(d),
                    )
                )
            )
        r_recv[step, pl.ds(me, 1)] = r_send[step][None]
        return copies

    def reduce_end(step, copies):
        for copy in copies:
            copy.wait_recv()
        count = (ny, nz)[step]
        return functools.reduce(jnp.add, [r_recv[step, n] for n in range(count)])

    reduced = reduce_start(0)

    def d_step(j, forward):
        later = []
        for h in range(HEADS):
            d_now[h].wait_recv()
            if forward:
                later.append(d_hop(j + 1, h))
        return later

    def from_far(j):
        for h in range(HEADS):
            scale = window_scale(h, D)
            grad = ds[j - 1, h]
            dv[h] = dv[h] + nn(p_far[j - 2, h], grad) * scale
            back_score = jnp.where(reach_k(h, j), nt(own[V, h], grad), 0.0).astype(BF)
            dk[h] = dk[h] + nn(back_score, qs[j - 1, h]) * scale

    def to_far(j):
        for h in range(HEADS):
            back_score = jnp.where(reach_q(h, j), nt(dm[h], kv[j - 1, V, h]), 0.0).astype(BF)
            dq[h] = dq[h] + nn(back_score, kv[j - 1, K, h]) * window_scale(h, D)

    def far_weight(j, h, n):
        at = (2 * h + n) * D
        return w_far[j - 1, :, at : at + D]

    d_now = d_step(1, True)
    across, near = across_start(1, scattered)
    even_f = 1.0 - odd_f
    states = []
    for h in range(HEADS):
        scale = window_scale(h, D) * any_after + far_weight(1, h, 0) * (even_f * level_scale(T))
        states.append(tn(qs[0, h], (scale * ds[0, h].astype(F32)).astype(BF)))
    to_far(2)

    d_now = d_step(2, True)
    to_far(3)
    gather = gather_start(1, across, near)
    from_far(2)

    d_now = d_step(3, True)
    reduced = reduce_end(0, reduced)
    r_send[1] = reduced
    reduced = reduce_start(1)
    to_far(4)
    for h in range(HEADS):
        dq_out[h] = dq[h].astype(BF)
    from_far(3)
    first_f = 1.0 - second_f
    for h in range(HEADS):
        for n in range(2):
            slot = 1 - odd + n
            at = (2 * h + 1) * D
            scale = w_far[slot, :, at : at + D] * (first_f * level_scale(2 * T))
            states[h] = states[h] + tn(
                qs[slot, h], (scale * ds[slot, h].astype(F32)).astype(BF)
            )

    for copy in gather:
        copy.wait_recv()
    d_step(4, False)
    from_far(4)
    for h in range(HEADS):
        state = (states[h] + gathered(1, h).astype(F32)).astype(BF)
        dk_out[h] = (dk[h] + nt(own[V, h], state)).astype(BF)
        dv_out[h] = (dv[h] + nn(own[K, h], state)).astype(BF)

    total = reduce_end(1, reduced)
    for h in range(HEADS):
        table_out[:, h] = total[8 * h : 8 * h + LEVELS, 0:ROWS]
    gain_out[...] = total[16 : 16 + HEADS]
    for copy in sent:
        copy.wait_send()


def shards(
    dims,
    query_rows,
    key_rows,
    value_rows,
    norm_gain,
    level_table,
    level_index,
    window_length,
    out_grad,
):
    big = jax.ShapeDtypeStruct((HEADS, T, D), BF)
    nz, ny, nh = dims
    vmem = pl.BlockSpec(memory_space=pltpu.VMEM)
    smem = pl.BlockSpec(memory_space=pltpu.SMEM)
    far = pl.BlockSpec(memory_space=pl.ANY)
    dma = pltpu.SemaphoreType.DMA
    layer, dq, dk, dv, table_grad, gain_grad = pl.pallas_call(
        functools.partial(kernel, dims),
        out_shape=(
            big,
            big,
            big,
            big,
            jax.ShapeDtypeStruct((LEVELS, HEADS, ROWS), F32),
            jax.ShapeDtypeStruct((HEADS, D), F32),
        ),
        in_specs=[far, far, far, far, vmem, smem, vmem, smem],
        out_specs=[vmem] * 6,
        scratch_shapes=[
            pltpu.VMEM((4, HEADS, T, D), BF),
            pltpu.VMEM((REACH, 2, HEADS, T, D), BF),
            pltpu.VMEM((REACH, HEADS, T, D), BF),
            pltpu.VMEM((REACH, HEADS, T, D), BF),
            pltpu.VMEM((3, 16, T), F32),
            pltpu.VMEM((16, T), F32),
            pltpu.VMEM((T, HEADS * LEVELS * D), F32),
            pltpu.VMEM((3, T, HEADS * 2 * D), F32),
            pltpu.VMEM((HEADS, T, T), F32),
            pltpu.VMEM((HEADS, T, T), F32),
            pltpu.VMEM((HEADS, T, T), BF),
            pltpu.VMEM((3, HEADS, T, T), BF),
            pltpu.VMEM((2, HEADS, D, D), BF),
            pltpu.VMEM((HEADS, T, D), F32),
            pltpu.VMEM((HEADS, T, D), BF),
            pltpu.VMEM((2, RING, HEADS, PIECE, D), BF),
            pltpu.VMEM((2, RING, HEADS, PIECE, D), BF),
            pltpu.VMEM((2, HEADS, PIECE, D), BF),
            pltpu.VMEM((2, nz, HEADS, PIECE, D), BF),
            pltpu.VMEM((2, 2, HEADS, PIECE, D), BF),
            pltpu.VMEM((2, RING, HEADS, PIECE, D), BF),
            pltpu.VMEM((8, T), F32),
            pltpu.VMEM((nh, 8, T), F32),
            pltpu.VMEM((2, 24, D), F32),
            pltpu.VMEM((2, RING, 24, D), F32),
            dma((4,)),
            dma((REACH, 2)),
            dma((REACH, 2)),
            dma((REACH,)),
            dma((REACH,)),
            dma((REACH, HEADS)),
            dma((REACH, HEADS)),
            dma((3,)),
            dma((3,)),
            dma((2, 3, RING)),
            dma((2, 3, RING)),
            dma((RING,)),
            dma((RING,)),
            dma((2, RING)),
            dma((2, RING)),
        ],
        compiler_params=pltpu.CompilerParams(
            collective_id=0, has_side_effects=True, vmem_limit_bytes=40 * 1024 * 1024
        ),
    )(
        query_rows,
        key_rows,
        value_rows,
        out_grad,
        norm_gain,
        jnp.transpose(level_table, (2, 1, 0)),
        level_index.T,
        window_length,
    )
    return layer, dq, dk, dv, jnp.transpose(table_grad, (2, 1, 0)), gain_grad


def solution(mesh):
    heads = mesh.shape["head"]
    dims = (mesh.shape["seq"] // RING, RING, heads)
    torus = Mesh(mesh.devices.reshape(*dims), ("seq_0", "seq_1", "head"))
    seq = ("seq_0", "seq_1")
    rows = P("head", seq, None)
    return jax.shard_map(
        functools.partial(shards, dims),
        mesh=torus,
        in_specs=(
            rows,
            rows,
            rows,
            P("head", None),
            P(None, "head", None),
            P(seq, None),
            P("head"),
            rows,
        ),
        out_specs=(rows, rows, rows, rows, P(None, "head", None), P("head", None)),
        check_vma=False,
    )
```

time: 330 us -> 84.1 us (0.25); the launches traced: 325 us -> 83.8 us
  waiting for transfers between devices: 93.1 us -> 0 us
  starting transfers between devices: 92.1 us -> 0 us
  Pallas kernels: 0 us -> 73.7 us
  blocking collectives: 43.7 us -> 0 us
  matrix products: 43.6 us -> 0 us
  other arithmetic: 20.8 us -> 0 us
  local copies, waits for them, and re-layouts: 26.9 us -> 9.45 us
    ppermute x20 -> x0, waiting for transfers between devices: 84.1 us -> none  [the longest x12 84.1 us: from_partner(): lax.ppermute(shard, axis, [(i, i ^ 1 << bit) for i in range(lax.axis_size...]
    ppermute x20 -> x0, starting transfers between devices: 83.9 us -> none  [the longest x12 51.5 us: from_partner(): lax.ppermute(shard, axis, [(i, i ^ 1 << bit) for i in range(lax.axis_size...]
    pallas_call x0 -> x1, Pallas kernels: none -> 73.7 us  [shards(): pl.pallas_call(functools.partial(kernel, dims), out_shape=(big, big, big,...]
    psum x2 -> x0, blocking collectives: 43.7 us -> none  [over_axes(): return functools.reduce(lax.psum, axes, shard)]
    dot_general x58 -> x0, matrix products: 43.6 us -> none  [the longest x56 42.6 us: contract(): jnp.einsum(pattern, left_side, right_side, preferred_element_type=jnp.flo...]
    all_to_all x2 -> x0, waiting for transfers between devices: 9 us -> none  [copy_for_each(): return lax.all_to_all(copies, axis, split_axis=0, concat_axis=0, tiled=True)]
    all_to_all x2 -> x0, starting transfers between devices: 8.24 us -> none  [copy_for_each(): return lax.all_to_all(copies, axis, split_axis=0, concat_axis=0, tiled=True)]
    reduce_sum x4 -> x0, other arithmetic: 6.95 us -> none  [the longest x1 2.72 us: shards(): jnp.sum(mixed_grad * area_list[level_no], axis=2)]
  transfers between devices with their start and end apart: 22 -> 0, of which waited for: 12 -> 0; matrix products, arithmetic and copies ran while one was open for 11% -> 0% of each run, Pallas kernels for 0% -> 0%
where the time goes in v1:
time: 84.1 us; the launch traced here: 83.8 us
  Pallas kernels  73.7 us (88%)
  local copies, waits for them, and re-layouts  9.45 us (11%)
    pallas_call x1, Pallas kernels, shards(): pl.pallas_call(functools.partial(kernel, dims), out_shape=(big, big, big,...  73.7 us
    unnamed x22, local copies, waits for them, and re-layouts  9.45 us

profile of v1, /device:TPU:56, one launch (start us, length us, event | category | flops | bytes accessed | tf_op | source)
XLA Modules:
  0.0 83.8 jit_solution(1292435644606688821)
XLA Ops:
  0.6 0.0 copy-start.6
  0.6 0.0 copy-start.7
  0.7 0.7 copy-done.6
  1.3 0.0 copy-done.7
  1.3 0.0 copy-start
  1.3 0.9 %copy-done = bf16[2,256,128]{2,1,0:T(8,128)(2,1)S(1)} copy-done((bf16[2,256,128]{2,1,0:T(8,128)(2,1)S(1)}, bf16[2,256,128]{2,1,0:T(8,128)(2,1)}, u32[]{:S(2)}) %copy-start) | copy-done | bytes 131096
  2.2 0.0 copy-start.1
  2.2 0.9 %copy-done.1 = bf16[2,256,128]{2,1,0:T(8,128)(2,1)S(1)} copy-done((bf16[2,256,128]{2,1,0:T(8,128)(2,1)S(1)}, bf16[2,256,128]{2,1,0:T(8,128)(2,1)}, u32[]{:S(2)}) %copy-start.1) | copy-done | bytes 131096
  3.1 0.0 copy-start.2
  3.1 0.9 %copy-done.2 = bf16[2,256,128]{2,1,0:T(8,128)(2,1)S(1)} copy-done((bf16[2,256,128]{2,1,0:T(8,128)(2,1)S(1)}, bf16[2,256,128]{2,1,0:T(8,128)(2,1)}, u32[]{:S(2)}) %copy-start.2) | copy-done | bytes 131096
  4.0 0.0 copy-start.3
  4.0 0.9 %copy-done.3 = bf16[2,256,128]{2,1,0:T(8,128)(2,1)S(1)} copy-done((bf16[2,256,128]{2,1,0:T(8,128)(2,1)S(1)}, bf16[2,256,128]{2,1,0:T(8,128)(2,1)}, u32[]{:S(2)}) %copy-start.3) | copy-done | bytes 131096
  4.9 0.0 copy-start.4
  4.9 0.7 copy-done.4
  5.6 0.0 copy-start.5
  5.6 0.7 copy-done.5
  6.3 73.7 %shard_map.127 = (bf16[2,256,128]{2,1,0:T(8,128)(2,1)S(1)}, bf16[2,256,128]{2,1,0:T(8,128)(2,1)S(1)}, bf16[2,256,128]{2,1,0:T(8,128)(2,1)S(1)}, bf16[2,256,128]{...) custom-call(bf16[2,256,128]{2,1,0:T(8,128)(2,1)S(1)} %copy-done, ...), custom_call_target="tpu_custom_call" | custom-call | tf_op jit(solution)/shard_map/pallas_call | solution.py:642
  80.0 0.7 copy.20
  80.7 0.7 copy.21
  81.4 0.7 copy.22
  82.0 0.7 copy.23
  82.7 0.6 copy.24
  83.3 0.6 copy.25
Async XLA Ops:
  0.6 0.7 copy-start.6
  0.6 0.7 copy-start.7
  1.3 0.9 %copy-start = (bf16[2,256,128]{2,1,0:T(8,128)(2,1)S(1)}, bf16[2,256,128]{2,1,0:T(8,128)(2,1)}, u32[]{:S(2)}) copy-start(bf16[2,256,128]{2,1,0:T(8,128)(2,1)} %q_in.1) | copy-start | bytes 393220
  2.2 0.9 %copy-start.1 = (bf16[2,256,128]{2,1,0:T(8,128)(2,1)S(1)}, bf16[2,256,128]{2,1,0:T(8,128)(2,1)}, u32[]{:S(2)}) copy-start(bf16[2,256,128]{2,1,0:T(8,128)(2,1)} %k_in.1) | copy-start | bytes 393220
  3.1 0.9 %copy-start.2 = (bf16[2,256,128]{2,1,0:T(8,128)(2,1)S(1)}, bf16[2,256,128]{2,1,0:T(8,128)(2,1)}, u32[]{:S(2)}) copy-start(bf16[2,256,128]{2,1,0:T(8,128)(2,1)} %v_in.1) | copy-start | bytes 393220
  4.0 0.9 %copy-start.3 = (bf16[2,256,128]{2,1,0:T(8,128)(2,1)S(1)}, bf16[2,256,128]{2,1,0:T(8,128)(2,1)}, u32[]{:S(2)}) copy-start(bf16[2,256,128]{2,1,0:T(8,128)(2,1)} %g_in.1) | copy-start | bytes 393220
  4.9 0.7 copy-start.4
  5.6 0.7 copy-start.5

commit v2 on v1

--- a/solution.py
+++ b/solution.py
@@ -55,16 +55,26 @@
     k_in,
     v_in,
     g_in,
-    gain,
-    table,
-    index,
-    window,
+    gain_in,
+    table_in,
+    index_in,
+    window_in,
+    out_to,
+    dq_to,
+    dk_to,
+    dv_to,
+    table_to,
+    gain_to,
     out,
     dq_out,
     dk_out,
     dv_out,
     table_out,
     gain_out,
+    gain,
+    table,
+    index,
+    window,
     own,
     kv,
     qs,
@@ -91,6 +101,7 @@
     r_send,
     r_recv,
     in_sem,
+    out_sem,
     kv_ss,
     kv_rs,
     q_ss,
@@ -105,6 +116,8 @@
     n_rs,
     r_ss,
     r_rs,
+    below,
+    above,
 ):
     nz, ny, nh = dims
     z = lax.axis_index("seq_0")
@@ -117,7 +130,7 @@
         return (z, lax.rem(y + d, ny), hd)
 
     def z_peer(d):
-        return (lax.rem(z + d, nz), y, hd)
+        return (lax.rem(z + d + nz, nz), y, hd)
 
     def h_peer(d):
         return (z, y, lax.rem(hd + d, nh))
@@ -133,22 +146,52 @@
 
     sent = []
 
-    def go(copy):
-        copy.start()
-        sent.append(copy)
+    def on(condition, action):
+        if condition is None:
+            action()
+        else:
+            pl.when(condition)(action)
+
+    def go(copy, condition=None):
+        on(condition, copy.start)
+        sent.append((copy, condition))
         return copy
 
+    results = (
+        (out, out_to),
+        (dq_out, dq_to),
+        (dk_out, dk_to),
+        (dv_out, dv_to),
+        (table_out, table_to),
+        (gain_out, gain_to),
+    )
+    stores = []
+
+    def store(n):
+        stores.append(pltpu.make_async_copy(*results[n], out_sem.at[n]))
+        stores[-1].start()
+
     barrier = pltpu.get_barrier_semaphore()
-    peers = [s_peer(1), s_peer(-1)]
-    peers += [y_peer(d) for d in range(1, ny)]
-    peers += [z_peer(d) for d in range(1, nz)]
-    peers += [h_peer(d) for d in range(1, nh)]
-    for peer in peers:
-        pl.semaphore_signal(barrier, inc=1, device_id=peer, device_id_type=MESH)
+    last = shard_count - 1
+    peers = [(s_peer(1), s < last), (s_peer(-1), s > 0)]
+    if nz > 1:
+        peers += [(z_peer(1), z < nz - 1), (z_peer(-1), z > 0)]
+    peers += [(y_peer(d), None) for d in range(1, ny)]
+    peers += [(h_peer(d), None) for d in range(1, nh)]
+
+    def signal(sem, peer):
+        pl.semaphore_signal(sem, inc=1, device_id=peer, device_id_type=MESH)
+
+    expected = 0
+    for peer, condition in peers:
+        on(condition, functools.partial(signal, barrier, peer))
+        expected = expected + (1 if condition is None else condition.astype(jnp.int32))
 
     loads = []
-    for n, ref in enumerate((k_in, v_in, q_in, g_in)):
-        load = pltpu.make_async_copy(ref, own.at[n], in_sem.at[n])
+    targets = (own.at[0], own.at[1], own.at[2], own.at[3], table, index, window, gain)
+    arrays = (k_in, v_in, q_in, g_in, table_in, index_in, window_in, gain_in)
+    for n, (ref, target) in enumerate(zip(arrays, targets)):
+        load = pltpu.make_async_copy(ref, target, in_sem.at[n])
         load.start()
         loads.append(load)
     loads[0].wait()
@@ -159,7 +202,21 @@
         state = tn(own[K, h], own[V, h])
         rs_send[0, :, h] = state.astype(BF).reshape(RING, PIECE, D)
 
-    pl.semaphore_wait(barrier, len(peers))
+    for j in range(1, REACH + 1):
+
+        def clear_before(j=j):
+            kv[j - 1] = jnp.zeros((2, HEADS, T, D), BF)
+
+        def clear_after(j=j):
+            qs[j - 1] = jnp.zeros((HEADS, T, D), BF)
+            ds[j - 1] = jnp.zeros((HEADS, T, D), BF)
+            if j < REACH:
+                ws[j - 1] = jnp.zeros((16, T), F32)
+
+        pl.when(s < j)(clear_before)
+        pl.when(s + j > last)(clear_after)
+
+    pl.semaphore_wait(barrier, expected)
 
     def scatter_start(side):
         copies = []
@@ -179,6 +236,12 @@
         rs_recv[side, pl.ds(y, 1)] = rs_send[side, pl.ds(y, 1)]
         return copies
 
+    def comes(side, d):
+        return z >= d if side == 0 else z + d < nz
+
+    def leaves(side, d):
+        return z + d < nz if side == 0 else z >= d
+
     def across_start(side, scattered):
         for copy in scattered:
             copy.wait_recv()
@@ -196,8 +259,9 @@
                         z_recv.at[side, d],
                         f_ss.at[side, 1, d],
                         f_rs.at[side, 1, d],
-                        z_peer(d),
-                    )
+                        z_peer(d if side == 0 else -d),
+                    ),
+                    leaves(side, d),
                 )
             )
         return copies, (low if side == 0 else upper)
@@ -205,9 +269,9 @@
     def gather_start(side, across, near):
         total = jnp.zeros((HEADS, PIECE, D), F32)
         for d in range(1, nz):
-            across[d - 1].wait_recv()
-            other = lax.rem(z - d + nz, nz)
-            counts = (other < z) if side == 0 else (other > z)
+            counts = comes(side, d)
+            on(counts, across[d - 1].wait_recv)
+            other = lax.rem((z - d if side == 0 else z + d) + nz, nz)
             scale = jnp.where(
                 lax.div(other, 2) == lax.div(z, 2),
                 level_scale(T * 8),
@@ -215,8 +279,7 @@
                     lax.div(other, 4) == lax.div(z, 4), level_scale(T * 16), level_scale(T * 32)
                 ),
             )
-            scale = jnp.where(counts, scale, 0.0)
-            total = total + z_recv[side, d].astype(F32) * scale
+            total = total + jnp.where(counts, z_recv[side, d].astype(F32) * scale, 0.0)
         with_near = (total + near * level_scale(T * 4)).astype(BF)
         plain = total.astype(BF)
         ag_send[side, 0] = plain if side == 0 else with_near
@@ -241,28 +304,53 @@
     def gathered(side, h):
         return ag_recv[side, :, h].reshape(D, D)
 
+    def before(j):
+        return s >= j
+
+    def after(j):
+        return s + j <= last
+
+    def forward(src, dst, ss, rs, j):
+        return go(remote(src, dst, ss, rs, s_peer(1)), (s >= j - 1) & (s < last))
+
+    def backward(src, dst, ss, rs, j):
+        return go(remote(src, dst, ss, rs, s_peer(-1)), (s + j - 1 <= last) & (s > 0))
+
     def kv_hop(j, c):
         src = (k_in, v_in)[c] if j == 1 else kv.at[j - 2, c]
-        return go(remote(src, kv.at[j - 1, c], kv_ss.at[j - 1, c], kv_rs.at[j - 1, c], s_peer(1)))
+        return forward(src, kv.at[j - 1, c], kv_ss.at[j - 1, c], kv_rs.at[j - 1, c], j)
 
     def q_hop(j):
         src = q_in if j == 1 else qs.at[j - 2]
-        return go(remote(src, qs.at[j - 1], q_ss.at[j - 1], q_rs.at[j - 1], s_peer(-1)))
+        return backward(src, qs.at[j - 1], q_ss.at[j - 1], q_rs.at[j - 1], j)
 
     def w_hop(j):
         src = w_own if j == 1 else ws.at[j - 2]
-        return go(remote(src, ws.at[j - 1], w_ss.at[j - 1], w_rs.at[j - 1], s_peer(-1)))
+        return backward(src, ws.at[j - 1], w_ss.at[j - 1], w_rs.at[j - 1], j)
 
     def d_hop(j, h):
         src = dm.at[h] if j == 1 else ds.at[j - 2, h]
-        return go(
-            remote(src, ds.at[j - 1, h], d_ss.at[j - 1, h], d_rs.at[j - 1, h], s_peer(-1))
-        )
+        return backward(src, ds.at[j - 1, h], d_ss.at[j - 1, h], d_rs.at[j - 1, h], j)
+
+    def kv_step(j, c):
+        on(before(j), kv_now[c].wait_recv)
+        if j < REACH:
+            kv_now[c] = kv_hop(j + 1, c)
+
+    def q_step(j):
+        on(after(j), q_now[0].wait_recv)
+        if j < REACH:
+            q_now[0] = q_hop(j + 1)
+            on(after(j), w_now[0].wait_recv)
+        if j < REACH - 1:
+            w_now[0] = w_hop(j + 1)
 
     scattered = scatter_start(0)
     kv_now = [kv_hop(1, K), kv_hop(1, V)]
-    q_now = q_hop(1)
-
+    q_now = [q_hop(1)]
+
+    for load in loads[2:]:
+        load.wait()
     index_row = index[...]
     for h in range(HEADS):
         rows = []
@@ -274,7 +362,7 @@
             rows.append(row)
         rows.append(jnp.zeros((8 - LEVELS, T), F32))
         w_own[8 * h : 8 * h + 8] = jnp.concatenate(rows, axis=0)
-    w_now = w_hop(1)
+    w_now = [w_hop(1)]
     spread = []
     for h in range(HEADS):
         for j in range(LEVELS):
@@ -300,8 +388,6 @@
     def twice(half):
         return jnp.concatenate([half, half], axis=1)
 
-    loads[2].wait()
-    loads[3].wait()
     for h in range(HEADS):
         raw = nt(own[Q, h], own[K, h])
         scale0 = twice(weight(h, 0) * level_scale(BLOCK))
@@ -344,77 +430,60 @@
     def near_scale(h, wide):
         return window_scale(h, D) * any_before + wide * (odd_f * level_scale(T))
 
+    def window_prob(h, j):
+        score = nt(own[Q, h], kv[j - 1, K, h])
+        return jnp.where(reach_q(h, j), score, 0.0).astype(BF)
+
     def window_part(h, j):
-        score = nt(own[Q, h], kv[j - 1, K, h])
-        prob = jnp.where(reach_q(h, j), score, 0.0).astype(BF)
-        return nn(prob, kv[j - 1, V, h]) * window_scale(h, D)
-
-    q_now.wait_recv()
-    q_now = q_hop(2)
-    w_now.wait_recv()
-    w_now = w_hop(2)
-    far_weights(1)
-
+        return nn(window_prob(h, j), kv[j - 1, V, h]) * window_scale(h, D)
+
+    if nz > 1:
+        on(z > 0, lambda: pl.semaphore_wait(below, 1))
+        on(z < nz - 1, lambda: signal(below, z_peer(1)))
+        for d in range(1, nz):
+            on(z >= d, functools.partial(signal, above, z_peer(-d)))
+
+    kv_step(1, K)
+    q_step(1)
+    kv_step(1, V)
+    if nz > 1:
+        on(z < nz - 1, lambda: pl.semaphore_wait(above, nz - 1 - z))
     across, near = across_start(0, scattered)
-
-    kv_now[K].wait_recv()
-    kv_next = [kv_hop(2, K)]
-    kv_now[V].wait_recv()
-    kv_next.append(kv_hop(2, V))
-    kv_now = kv_next
     for h in range(HEADS):
         state = tn(kv[0, K, h], kv[0, V, h]).astype(BF)
         s_near[0, h] = state
         mix[h] = mix[h] + near_scale(h, weight(h, 3)) * nn(own[Q, h], state)
 
-    q_now.wait_recv()
-    q_now = q_hop(3)
-    w_now.wait_recv()
-    w_now = w_hop(3)
+    kv_step(2, K)
+    q_step(2)
+    far_weights(1)
+    kv_step(2, V)
+    gather = gather_start(0, across, near)
+    for h in range(HEADS):
+        mix[h] = mix[h] + window_part(h, 2)
+
+    kv_step(3, K)
+    q_step(3)
     far_weights(2)
     far_probs(2)
-
-    gather = gather_start(0, across, near)
-
-    kv_now[K].wait_recv()
-    kv_next = [kv_hop(3, K)]
-    kv_now[V].wait_recv()
-    kv_next.append(kv_hop(3, V))
-    kv_now = kv_next
-    for h in range(HEADS):
-        mix[h] = mix[h] + window_part(h, 2)
-
-    q_now.wait_recv()
-    q_now = q_hop(4)
-    w_now.wait_recv()
-    far_weights(3)
-    far_probs(3)
-
-    for copy in gather:
-        copy.wait_recv()
-    for h in range(HEADS):
-        mix[h] = mix[h] + weight(h, 5) * nn(own[Q, h], gathered(0, h))
-
-    kv_now[K].wait_recv()
-    kv_next = [kv_hop(4, K)]
-    kv_now[V].wait_recv()
-    kv_next.append(kv_hop(4, V))
-    kv_now = kv_next
+    kv_step(3, V)
     for h in range(HEADS):
         state = tn(kv[odd, K, h], kv[odd, V, h]) + tn(kv[odd + 1, K, h], kv[odd + 1, V, h])
         state = (state * (second_f * level_scale(2 * T))).astype(BF)
         s_near[1, h] = state
         mix[h] = mix[h] + window_part(h, 3) + weight(h, 4) * nn(own[Q, h], state)
-
-    q_now.wait_recv()
-    far_probs(4)
-
-    kv_now[K].wait_recv()
-    kv_now[V].wait_recv()
+    for copy in gather:
+        copy.wait_recv()
+    for h in range(HEADS):
+        mix[h] = mix[h] + weight(h, 5) * nn(own[Q, h], gathered(0, h))
+
+    kv_step(4, K)
+    last_probs = [window_prob(h, 4) for h in range(HEADS)]
+    kv_step(4, V)
     square = jnp.zeros((T, D), F32)
     cross = jnp.zeros((T, D), F32)
     for h in range(HEADS):
-        mixed = mix[h] + window_part(h, 4)
+        mixed = mix[h] + nn(last_probs[h], kv[3, V, h]) * window_scale(h, D)
         mix[h] = mixed
         square = square + mixed * mixed
         cross = cross + own[G, h].astype(F32) * gain[h : h + 1] * mixed
@@ -436,25 +505,26 @@
     inv_rms = wide[:, :D]
     back = wide[:, D:]
 
-    d_now = []
     grads = []
     for h in range(HEADS):
         given = own[G, h].astype(F32)
         grad = given * gain[h : h + 1] * inv_rms - mix[h] * back
         dm[h] = grad.astype(BF)
         grads.append(grad)
-        d_now.append(d_hop(1, h))
     for h in range(HEADS):
         up = (weight(h, 5) * grads[h]).astype(BF)
         state = tn(own[Q, h], up)
         rs_send[1, :, h] = state.astype(BF).reshape(RING, PIECE, D)
     scattered = scatter_start(1)
+    d_now = [d_hop(1, h) for h in range(HEADS)]
 
     gain_rows = []
     for h in range(HEADS):
         scaled = mix[h] * inv_rms
         out[h] = (scaled * gain[h : h + 1]).astype(BF)
         gain_rows.append(jnp.sum(own[G, h].astype(F32) * scaled, axis=0, keepdims=True))
+
+    store(0)
 
     lane_block = iota((8, T), 1) >> 6
     row_no = iota((8, T), 0)
@@ -548,13 +618,11 @@
 
     reduced = reduce_start(0)
 
-    def d_step(j, forward):
-        later = []
+    def d_step(j):
         for h in range(HEADS):
-            d_now[h].wait_recv()
-            if forward:
-                later.append(d_hop(j + 1, h))
-        return later
+            on(after(j), d_now[h].wait_recv)
+            if j < REACH:
+                d_now[h] = d_hop(j + 1, h)
 
     def from_far(j):
         for h in range(HEADS):
@@ -573,8 +641,10 @@
         at = (2 * h + n) * D
         return w_far[j - 1, :, at : at + D]
 
-    d_now = d_step(1, True)
+    d_step(1)
     across, near = across_start(1, scattered)
+    far_weights(3)
+    far_probs(3)
     even_f = 1.0 - odd_f
     states = []
     for h in range(HEADS):
@@ -582,18 +652,19 @@
         states.append(tn(qs[0, h], (scale * ds[0, h].astype(F32)).astype(BF)))
     to_far(2)
 
-    d_now = d_step(2, True)
+    d_step(2)
+    r_send[1] = reduce_end(0, reduced)
+    reduced = reduce_start(1)
     to_far(3)
-    gather = gather_start(1, across, near)
     from_far(2)
 
-    d_now = d_step(3, True)
-    reduced = reduce_end(0, reduced)
-    r_send[1] = reduced
-    reduced = reduce_start(1)
+    d_step(3)
+    q_step(4)
+    far_probs(4)
     to_far(4)
     for h in range(HEADS):
         dq_out[h] = dq[h].astype(BF)
+    store(1)
     from_far(3)
     first_f = 1.0 - second_f
     for h in range(HEADS):
@@ -605,21 +676,33 @@
                 qs[slot, h], (scale * ds[slot, h].astype(F32)).astype(BF)
             )
 
+    d_step(4)
+    from_far(4)
+    gather = gather_start(1, across, near)
     for copy in gather:
         copy.wait_recv()
-    d_step(4, False)
-    from_far(4)
     for h in range(HEADS):
         state = (states[h] + gathered(1, h).astype(F32)).astype(BF)
         dk_out[h] = (dk[h] + nt(own[V, h], state)).astype(BF)
         dv_out[h] = (dv[h] + nn(own[K, h], state)).astype(BF)
 
+    store(2)
+    store(3)
     total = reduce_end(1, reduced)
     for h in range(HEADS):
         table_out[:, h] = total[8 * h : 8 * h + LEVELS, 0:ROWS]
     gain_out[...] = total[16 : 16 + HEADS]
-    for copy in sent:
-        copy.wait_send()
+    store(4)
+    store(5)
+    for copy, condition in sent:
+        on(condition, copy.wait_send)
+    for copy in stores:
+        copy.wait()
+
+
+def place_kernel(*refs):
+    for n in range(6):
+        refs[6 + n][...] = refs[n][...]
 
 
 def shards(
@@ -635,11 +718,10 @@
 ):
     big = jax.ShapeDtypeStruct((HEADS, T, D), BF)
     nz, ny, nh = dims
+    far = pl.BlockSpec(memory_space=pl.ANY)
     vmem = pl.BlockSpec(memory_space=pltpu.VMEM)
-    smem = pl.BlockSpec(memory_space=pltpu.SMEM)
-    far = pl.BlockSpec(memory_space=pl.ANY)
     dma = pltpu.SemaphoreType.DMA
-    layer, dq, dk, dv, table_grad, gain_grad = pl.pallas_call(
+    results = pl.pallas_call(
         functools.partial(kernel, dims),
         out_shape=(
             big,
@@ -649,9 +731,19 @@
             jax.ShapeDtypeStruct((LEVELS, HEADS, ROWS), F32),
             jax.ShapeDtypeStruct((HEADS, D), F32),
         ),
-        in_specs=[far, far, far, far, vmem, smem, vmem, smem],
-        out_specs=[vmem] * 6,
+        in_specs=[far] * 8,
+        out_specs=[far] * 6,
         scratch_shapes=[
+            pltpu.VMEM((HEADS, T, D), BF),
+            pltpu.VMEM((HEADS, T, D), BF),
+            pltpu.VMEM((HEADS, T, D), BF),
+            pltpu.VMEM((HEADS, T, D), BF),
+            pltpu.VMEM((LEVELS, HEADS, ROWS), F32),
+            pltpu.VMEM((HEADS, D), F32),
+            pltpu.VMEM((HEADS, D), F32),
+            pltpu.SMEM((LEVELS, HEADS, ROWS), F32),
+            pltpu.VMEM((LEVELS, T), jnp.int32),
+            pltpu.SMEM((HEADS,), jnp.int32),
             pltpu.VMEM((4, HEADS, T, D), BF),
             pltpu.VMEM((REACH, 2, HEADS, T, D), BF),
             pltpu.VMEM((REACH, HEADS, T, D), BF),
@@ -677,7 +769,8 @@
             pltpu.VMEM((nh, 8, T), F32),
             pltpu.VMEM((2, 24, D), F32),
             pltpu.VMEM((2, RING, 24, D), F32),
-            dma((4,)),
+            dma((8,)),
+            dma((6,)),
             dma((REACH, 2)),
             dma((REACH, 2)),
             dma((REACH,)),
@@ -692,9 +785,11 @@
             dma((RING,)),
             dma((2, RING)),
             dma((2, RING)),
+            pltpu.SemaphoreType.REGULAR,
+            pltpu.SemaphoreType.REGULAR,
         ],
         compiler_params=pltpu.CompilerParams(
-            collective_id=0, has_side_effects=True, vmem_limit_bytes=40 * 1024 * 1024
+            collective_id=0, has_side_effects=True, vmem_limit_bytes=56 * 1024 * 1024
         ),
     )(
         query_rows,
@@ -706,6 +801,12 @@
         level_index.T,
         window_length,
     )
+    layer, dq, dk, dv, table_grad, gain_grad = pl.pallas_call(
+        place_kernel,
+        out_shape=[jax.ShapeDtypeStruct(r.shape, r.dtype) for r in results],
+        in_specs=[vmem] * 6,
+        out_specs=[vmem] * 6,
+    )(*results)
     return layer, dq, dk, dv, jnp.transpose(table_grad, (2, 1, 0)), gain_grad
 
 

time: 84.1 us -> 72.9 us (0.87)
  the two profiles are of different devices: /device:TPU:56 before, /device:TPU:320 now
where the time goes in v2:
time: 72.9 us; the launch traced here: 72.8 us
  Pallas kernels  72.1 us (99%)
    pallas_call x1, Pallas kernels, shards(): pl.pallas_call(functools.partial(kernel, dims), out_shape=(big, big, big,...  70.2 us
    pallas_call x1, Pallas kernels, shards(): pl.pallas_call(place_kernel, out_shape=[jax.ShapeDtypeStruct(r.shape, r.d...  1.9 us

profile of v2, /device:TPU:320, one launch (start us, length us, event | category | flops | bytes accessed | tf_op | source)
XLA Modules:
  0.0 72.8 jit_solution(2049226037883336013)
XLA Ops:
  0.6 70.2 %shard_map.127 = (bf16[2,256,128]{2,1,0:T(8,128)(2,1)}, bf16[2,256,128]{2,1,0:T(8,128)(2,1)}, bf16[2,256,128]{2,1,0:T(8,128)(2,1)}, bf16[2,256,128]{2,1,0:T(8,12...) custom-call(bf16[2,256,128]{2,1,0:T(8,128)(2,1)} %q_in.1, bf16[2,256,128]{2,1,0:T(8,128)(2,1)} %k_in.1, ...), custom_call_target="tpu_custom_call" | custom-call | tf_op jit(solution)/shard_map/pallas_call | solution.py:724
  70.9 1.9 %shard_map.128 = (bf16[2,256,128]{2,1,0:T(8,128)(2,1)}, bf16[2,256,128]{2,1,0:T(8,128)(2,1)}, bf16[2,256,128]{2,1,0:T(8,128)(2,1)}, bf16[2,256,128]{2,1,0:T(8,12...) custom-call(bf16[2,256,128]{2,1,0:T(8,128)(2,1)} %get-tuple-element.18.refs_0_, ...), custom_call_target="tpu_custom_call" | custom-call | tf_op jit(solution)/shard_map/pallas_call | solution.py:804

commit v3 on v2

--- a/solution.py
+++ b/solution.py
@@ -21,7 +21,6 @@
 EPS = 1e-06
 BF = jnp.bfloat16
 F32 = jnp.float32
-HIGH = lax.Precision.HIGHEST
 MESH = pl.DeviceIdType.MESH
 
 
@@ -33,16 +32,27 @@
     return lax.dot_general(a, b, (((1,), (0,)), ((), ())), preferred_element_type=F32)
 
 
-def nt(a, b, precision=None):
-    return lax.dot_general(
-        a, b, (((1,), (1,)), ((), ())), precision=precision, preferred_element_type=F32
-    )
-
-
-def tn(a, b, precision=None):
-    return lax.dot_general(
-        a, b, (((0,), (0,)), ((), ())), precision=precision, preferred_element_type=F32
-    )
+def nt(a, b):
+    return lax.dot_general(a, b, (((1,), (1,)), ((), ())), preferred_element_type=F32)
+
+
+def tn(a, b):
+    return lax.dot_general(a, b, (((0,), (0,)), ((), ())), preferred_element_type=F32)
+
+
+def halves(x):
+    high = x.astype(BF)
+    return high, (x - high.astype(F32)).astype(BF)
+
+
+def pick_nt(ones, x):
+    high, low = halves(x)
+    return nt(ones, high) + nt(ones, low)
+
+
+def pick_tn(x, ones):
+    high, low = halves(x)
+    return tn(high, ones) + tn(low, ones)
 
 
 def iota(shape, dim):
@@ -366,8 +376,8 @@
     spread = []
     for h in range(HEADS):
         for j in range(LEVELS):
-            spread.append((iota((16, D), 0) == 8 * h + j).astype(F32))
-    w_wide[...] = tn(w_own[...], jnp.concatenate(spread, axis=1), HIGH)
+            spread.append((iota((16, D), 0) == 8 * h + j).astype(BF))
+    w_wide[...] = pick_tn(w_own[...], jnp.concatenate(spread, axis=1))
 
     def weight(h, j):
         at = (h * LEVELS + j) * D
@@ -418,8 +428,8 @@
         spread = []
         for h in range(HEADS):
             for n in (3, 4):
-                spread.append((iota((16, D), 0) == 8 * h + n).astype(F32))
-        w_far[j - 1] = tn(ws[j - 1], jnp.concatenate(spread, axis=1), HIGH)
+                spread.append((iota((16, D), 0) == 8 * h + n).astype(BF))
+        w_far[j - 1] = pick_tn(ws[j - 1], jnp.concatenate(spread, axis=1))
 
     odd = lax.rem(s, 2)
     odd_f = odd.astype(F32)
@@ -489,8 +499,8 @@
         cross = cross + own[G, h].astype(F32) * gain[h : h + 1] * mixed
 
     both = jnp.concatenate([square, cross], axis=1)
-    pick = (iota((8, 2 * D), 0) == (iota((8, 2 * D), 1) >> 7)).astype(F32)
-    n_send[...] = nt(pick, both, HIGH)
+    pick = (iota((16, 2 * D), 0) == (iota((16, 2 * D), 1) >> 7)).astype(BF)
+    n_send[...] = pick_nt(pick, both)[0:8]
     norms = []
     for d in range(1, nh):
         norms.append(go(remote(n_send, n_recv.at[hd], n_ss.at[d], n_rs.at[d], h_peer(d))))
@@ -500,8 +510,8 @@
     sums = functools.reduce(jnp.add, [n_recv[n] for n in range(nh)])
     inv_row = lax.rsqrt(sums[0:1] * (1.0 / (HEADS * nh * D)) + EPS)
     back_row = inv_row * inv_row * inv_row * sums[1:2] * (1.0 / (HEADS * nh * D))
-    both_rows = jnp.concatenate([inv_row, back_row, jnp.zeros((6, T), F32)], axis=0)
-    wide = tn(both_rows, pick, HIGH)
+    both_rows = jnp.concatenate([inv_row, back_row, jnp.zeros((14, T), F32)], axis=0)
+    wide = pick_tn(both_rows, pick)
     inv_rms = wide[:, :D]
     back = wide[:, D:]
 
@@ -521,37 +531,25 @@
     gain_rows = []
     for h in range(HEADS):
         scaled = mix[h] * inv_rms
-        out[h] = (scaled * gain[h : h + 1]).astype(BF)
         gain_rows.append(jnp.sum(own[G, h].astype(F32) * scaled, axis=0, keepdims=True))
-
-    store(0)
 
     lane_block = iota((8, T), 1) >> 6
     row_no = iota((8, T), 0)
+    block_ones = (iota((16, T), 0) == (iota((16, T), 1) >> 6)).astype(BF)
     hot = jnp.concatenate(
-        [(index_row[j : j + 1] == iota((ROWS, T), 0)).astype(F32) for j in range(LEVELS)], axis=0
+        [(index_row[j : j + 1] == iota((ROWS, T), 0)).astype(BF) for j in range(LEVELS)], axis=0
     )
     dq = []
     dk = []
     dv = []
+    score_grads = []
     for h in range(HEADS):
         grad = grads[h]
         low = dm[h]
         prob_grad = nt(low, own[V, h])
         product = jnp.where(causal, p_raw[h] * prob_grad, 0.0)
-        score_grad = (prob_grad * a_mix[h]).astype(BF)
-        dk.append(tn(score_grad, own[Q, h]))
-        dv.append(tn(p_low[h], low))
-        up1 = (near_scale(h, weight(h, 3)) * grad).astype(BF)
-        up4 = (weight(h, 4) * grad).astype(BF)
-        up5 = (weight(h, 5) * grad).astype(BF)
-        dq.append(
-            nn(score_grad, own[K, h])
-            + nt(up1, s_near[0, h])
-            + nt(up4, s_near[1, h])
-            + nt(up5, gathered(0, h))
-        )
-        by_block = nt((row_no == lane_block).astype(F32), product, HIGH)
+        score_grads.append((prob_grad * a_mix[h]).astype(BF))
+        by_block = pick_nt(block_ones, product)[0:8]
         row0 = jnp.sum(jnp.where(row_no == lane_block, by_block, 0.0), axis=0, keepdims=True)
         row1 = jnp.sum(
             jnp.where((row_no == lane_block - 1) & ((lane_block & 1) == 1), by_block, 0.0),
@@ -569,19 +567,20 @@
             ],
             axis=1,
         )
-        pick3 = (iota((8, 3 * D), 0) == (iota((8, 3 * D), 1) >> 7)).astype(F32)
-        far_rows = nt(pick3, areas, HIGH)
+        pick3 = (iota((16, 3 * D), 0) == (iota((16, 3 * D), 1) >> 7)).astype(BF)
+        far_rows = pick_nt(pick3, areas)
         weight_rows = jnp.concatenate(
             [
                 row0 * level_scale(BLOCK),
                 row1 * level_scale(BLOCK),
                 row2 * level_scale(2 * BLOCK),
                 far_rows[0:3],
-                jnp.zeros((2, T), F32),
+                jnp.zeros((10, T), F32),
             ],
             axis=0,
         )
-        by_level = nt(weight_rows, hot, HIGH)
+        high, rest = halves(weight_rows)
+        by_level = (nt(high, hot) + nt(rest, hot))[0:8]
         part = jnp.zeros((8, ROWS), F32)
         for j in range(LEVELS):
             slab = by_level[:, ROWS * j : ROWS * (j + 1)]
@@ -617,6 +616,22 @@
         return functools.reduce(jnp.add, [r_recv[step, n] for n in range(count)])
 
     reduced = reduce_start(0)
+    across, near = across_start(1, scattered)
+
+    for h in range(HEADS):
+        grad = grads[h]
+        out[h] = (mix[h] * inv_rms * gain[h : h + 1]).astype(BF)
+        dk.append(tn(score_grads[h], own[Q, h]))
+        dv.append(tn(p_low[h], dm[h]))
+        up1 = (near_scale(h, weight(h, 3)) * grad).astype(BF)
+        up4 = (weight(h, 4) * grad).astype(BF)
+        up5 = (weight(h, 5) * grad).astype(BF)
+        dq.append(
+            nn(score_grads[h], own[K, h])
+            + nt(up1, s_near[0, h])
+            + nt(up4, s_near[1, h])
+            + nt(up5, gathered(0, h))
+        )
 
     def d_step(j):
         for h in range(HEADS):
@@ -641,8 +656,8 @@
         at = (2 * h + n) * D
         return w_far[j - 1, :, at : at + D]
 
+    store(0)
     d_step(1)
-    across, near = across_start(1, scattered)
     far_weights(3)
     far_probs(3)
     even_f = 1.0 - odd_f
@@ -652,9 +667,9 @@
         states.append(tn(qs[0, h], (scale * ds[0, h].astype(F32)).astype(BF)))
     to_far(2)
 
-    d_step(2)
     r_send[1] = reduce_end(0, reduced)
     reduced = reduce_start(1)
+    d_step(2)
     to_far(3)
     from_far(2)
 
@@ -676,9 +691,9 @@
                 qs[slot, h], (scale * ds[slot, h].astype(F32)).astype(BF)
             )
 
+    gather = gather_start(1, across, near)
     d_step(4)
     from_far(4)
-    gather = gather_start(1, across, near)
     for copy in gather:
         copy.wait_recv()
     for h in range(HEADS):
@@ -701,8 +716,16 @@
 
 
 def place_kernel(*refs):
-    for n in range(6):
-        refs[6 + n][...] = refs[n][...]
+    arrays, targets, rest, (in_sem, out_sem) = refs[:6], refs[6:12], refs[12:18], refs[18:]
+    loads = [pltpu.make_async_copy(arrays[n], rest[n], in_sem.at[n]) for n in range(6)]
+    stores = [pltpu.make_async_copy(rest[n], targets[n], out_sem.at[n]) for n in range(6)]
+    for load in loads:
+        load.start()
+    for load, store in zip(loads, stores):
+        load.wait()
+        store.start()
+    for store in stores:
+        store.wait()
 
 
 def shards(
@@ -719,7 +742,6 @@
     big = jax.ShapeDtypeStruct((HEADS, T, D), BF)
     nz, ny, nh = dims
     far = pl.BlockSpec(memory_space=pl.ANY)
-    vmem = pl.BlockSpec(memory_space=pltpu.VMEM)
     dma = pltpu.SemaphoreType.DMA
     results = pl.pallas_call(
         functools.partial(kernel, dims),
@@ -804,8 +826,10 @@
     layer, dq, dk, dv, table_grad, gain_grad = pl.pallas_call(
         place_kernel,
         out_shape=[jax.ShapeDtypeStruct(r.shape, r.dtype) for r in results],
-        in_specs=[vmem] * 6,
-        out_specs=[vmem] * 6,
+        in_specs=[far] * 6,
+        out_specs=[far] * 6,
+        scratch_shapes=[pltpu.VMEM(r.shape, r.dtype) for r in results] + [dma((6,)), dma((6,))],
+        compiler_params=pltpu.CompilerParams(vmem_limit_bytes=56 * 1024 * 1024),
     )(*results)
     return layer, dq, dk, dv, jnp.transpose(table_grad, (2, 1, 0)), gain_grad
 

time: 72.9 us -> 69.6 us (0.955)
  the two profiles are of different devices: /device:TPU:320 before, /device:TPU:120 now
where the time goes in v3:
time: 69.6 us; the launch traced here: 69.5 us
  Pallas kernels  68.8 us (99%)
    pallas_call x1, Pallas kernels, shards(): pl.pallas_call(functools.partial(kernel, dims), out_shape=(big, big, big,...  67 us
    pallas_call x1, Pallas kernels, shards(): pl.pallas_call(place_kernel, out_shape=[jax.ShapeDtypeStruct(r.shape, r.d...  1.86 us

profile of v3, /device:TPU:120, one launch (start us, length us, event | category | flops | bytes accessed | tf_op | source)
XLA Modules:
  0.0 69.5 jit_solution(10712100541291689704)
XLA Ops:
  0.6 67.0 %shard_map.127 = (bf16[2,256,128]{2,1,0:T(8,128)(2,1)}, bf16[2,256,128]{2,1,0:T(8,128)(2,1)}, bf16[2,256,128]{2,1,0:T(8,128)(2,1)}, bf16[2,256,128]{2,1,0:T(8,12...) custom-call(bf16[2,256,128]{2,1,0:T(8,128)(2,1)} %q_in.1, bf16[2,256,128]{2,1,0:T(8,128)(2,1)} %k_in.1, ...), custom_call_target="tpu_custom_call" | custom-call | tf_op jit(solution)/shard_map/pallas_call | solution.py:746
  67.6 1.9 %shard_map.128 = (bf16[2,256,128]{2,1,0:T(8,128)(2,1)}, bf16[2,256,128]{2,1,0:T(8,128)(2,1)}, bf16[2,256,128]{2,1,0:T(8,128)(2,1)}, bf16[2,256,128]{2,1,0:T(8,12...) custom-call(bf16[2,256,128]{2,1,0:T(8,128)(2,1)} %get-tuple-element.18.refs_0_, ...), custom_call_target="tpu_custom_call" | custom-call | tf_op jit(solution)/shard_map/pallas_call | solution.py:826
